TPU v7x, 512 devices: a whole 4x4x16 slice. The times are simulated.
512 devices in a mesh: gz: 32 (over z, core), gy: 4 (over y), gx: 4 (over x).
Axes of the slice: x: 4, y: 4, z: 16, core: 2. Of those that a mesh axis runs over, the one named last changes fastest.
Arguments:
- pressure: float32 [128, 512, 512], P('gz', 'gy', 'gx'), may hold values from -6 to 6
- light: float32 [4, 3], replicated, may hold values from -4 to 4
- palette: float32 [3, 2], replicated, may hold values from -4 to 4
- rate: float32 [4], replicated, may hold values from 0.00390625 to 0.0234375
- shear: int32 [4, 128, 2], replicated, may hold values from 0 to 8
- offset: int32 [4, 32, 2], replicated, may hold values from 0 to 31
- order: int32 [4, 32], replicated, may hold values from 0 to 31, each once within a row
Outputs:
- picture: float32 [4, 4, 32, 16, 512], P(None, None, 'gz', 'gy', 'gx')
Inputs may be any that keep to these rules, and one draw needn't show every extreme that they name: `order`: each row is a permutation of 0 to 31.
All inputs are finite; a program needn't handle non-finite values.
Results may differ from a plain program's by a relative error of at most 0.00005.
Values sent between devices are 32-bit elements; how exact they have to be, the bound alone decides.
No kernel may reach another device: no remote copies, remote signals or barrier semaphores. Data moves between devices by JAX's collectives and lax.ppermute only.
A program may use at most 64 MiB of HBM per device.

v0:
```python
import jax
import jax.numpy as jnp
from jax import lax
from jax.sharding import PartitionSpec as P

VIEWS = 4
SHEAR = 8
REACH = 32


def padded(cells, sides, width):
    for axis, dim in sides:
        count = lax.axis_size(axis)
        ends = count - 1
        head = lax.slice_in_dim(cells, 0, width, axis=dim)
        tail = lax.slice_in_dim(cells, cells.shape[dim] - width, cells.shape[dim], axis=dim)
        cells = jnp.concatenate(
            [
                lax.ppermute(tail, axis, [(i, (i + 1) % count) for i in range(ends)]),
                cells,
                lax.ppermute(head, axis, [((i + 1) % count, i) for i in range(ends)]),
            ],
            axis=dim,
        )
    return cells


def shifted(value, axis, steps):
    count = lax.axis_size(axis)
    first, last = (max(0, -steps), min(count, count - steps))
    return lax.ppermute(value, axis, [(source, source + steps) for source in range(first, last)])


def surface_terms(slab):
    inner = slab[1:-1, 1:-1, 1:-1]
    grad_depth = 0.5 * (slab[2:, 1:-1, 1:-1] - slab[:-2, 1:-1, 1:-1])
    grad_rows = 0.5 * (slab[1:-1, 2:, 1:-1] - slab[1:-1, :-2, 1:-1])
    grad_cols = 0.5 * (slab[1:-1, 1:-1, 2:] - slab[1:-1, 1:-1, :-2])
    factor = lax.rsqrt(
        grad_depth * grad_depth + grad_rows * grad_rows + grad_cols * grad_cols + 1.0
    )
    return (inner, (grad_depth * factor, grad_rows * factor, grad_cols * factor))


def render_layers(inner, normals, shifts, light, palette, rate, rows, cols):
    lengths = jnp.sqrt(jnp.sum(light * light, axis=1, keepdims=True) + 1.0)
    towards = light / lengths
    offsets = palette[:, 0][:, None, None]
    slopes = palette[:, 1][:, None, None]
    layers = []
    for view in range(light.shape[0]):

        def advance(carry, items):
            color, depth = carry
            value_slab, normal_depth, normal_rows, normal_cols, moved = items
            start = (SHEAR - moved[0], SHEAR - moved[1])
            value = lax.dynamic_slice(value_slab, start, (rows, cols))
            dot = (
                lax.dynamic_slice(normal_depth, start, (rows, cols)) * towards[view, 0]
                + lax.dynamic_slice(normal_rows, start, (rows, cols)) * towards[view, 1]
                + lax.dynamic_slice(normal_cols, start, (rows, cols)) * towards[view, 2]
            )
            shade = 0.25 + 0.75 * dot * dot
            density = rate[view] * (1.0 + jnp.tanh(value))
            alpha = 1.0 - jnp.exp(-density)
            weight = alpha * jnp.exp(-depth)
            hues = jax.nn.sigmoid(offsets + slopes * value[None]) * shade[None]
            return ((color + hues * weight[None], depth + density), None)

        start_carry = (
            jnp.zeros((3, rows, cols), jnp.float32),
            jnp.zeros((rows, cols), jnp.float32),
        )
        (color, depth), _ = lax.scan(
            advance, start_carry, (inner, normals[0], normals[1], normals[2], shifts[view])
        )
        layers.append(jnp.concatenate([color, depth[None]], axis=0))
    return jnp.stack(layers)


def precedence(order):
    bricks = order.shape[1]
    onehot = (order[:, :, None] == jnp.arange(bricks, dtype=jnp.int32)[None, None, :]).astype(
        jnp.float32
    )
    ranks = jnp.sum(onehot * jnp.arange(bricks, dtype=jnp.float32)[None, :, None], axis=1)
    return (ranks[:, None, :] < ranks[:, :, None]).astype(jnp.float32)


def on_device(pressure, light, palette, rate, shear, offset, order):
    depth_cells, rows, cols = pressure.shape
    brick = lax.axis_index("gz")
    zero = jnp.zeros((), jnp.int32)
    widened = padded(pressure, (("gy", 1), ("gx", 2)), SHEAR + 1)
    slab = padded(widened, (("gz", 0),), 1)
    inner, normals = surface_terms(slab)
    shifts = lax.dynamic_slice(shear, (zero, brick * depth_cells, zero), (VIEWS, depth_cells, 2))
    layers = render_layers(inner, normals, shifts, light, palette, rate, rows, cols)
    moved = lax.dynamic_index_in_dim(offset, brick, 1, keepdims=False)
    blank = jnp.zeros((4, rows + REACH, cols + REACH), jnp.float32)
    canvas = jnp.stack(
        [
            lax.dynamic_update_slice(blank, layers[view], (zero, moved[view, 0], moved[view, 1]))
            for view in range(VIEWS)
        ]
    )
    own_tile = canvas[:, :, :rows, :cols]
    from_above = shifted(canvas[:, :, rows:, :cols], "gy", 1)
    from_left = shifted(canvas[:, :, :rows, cols:], "gx", 1)
    from_diagonal = shifted(canvas[:, :, rows:, cols:], ("gy", "gx"), lax.axis_size("gx") + 1)
    from_diagonal = from_diagonal * (lax.axis_index("gx") > 0).astype(jnp.float32)
    own_tile = own_tile.at[:, :, :REACH, :].add(from_above)
    own_tile = own_tile.at[:, :, :, :REACH].add(from_left)
    own_tile = own_tile.at[:, :, :REACH, :REACH].add(from_diagonal)
    ranking = precedence(order)
    pieces = lax.all_to_all(own_tile[None], "gz", split_axis=3, concat_axis=0, tiled=True)
    depths = pieces[:, :, 3]
    cover = jnp.einsum("vbc,cvyx->bvyx", ranking, depths, precision=lax.Precision.HIGHEST)
    colors = jnp.sum(pieces[:, :, :3] * jnp.exp(-cover)[:, :, None], axis=0)
    opacity = 1.0 - jnp.exp(-jnp.sum(depths, axis=0))
    image = jnp.concatenate([colors, opacity[:, None]], axis=1)
    return image[:, :, None]


def solution(mesh):
    return jax.shard_map(
        on_device,
        mesh=mesh,
        in_specs=(P("gz", "gy", "gx"), P(), P(), P(), P(), P(), P()),
        out_specs=P(None, None, "gz", "gy", "gx"),
        check_vma=False,
    )
```

profile of v0, /device:TPU:27, one launch (start us, length us, event | category | flops | bytes accessed | tf_op | source)
XLA Modules:
  0.0 283.3 jit_solution(8438812857838250541)
XLA Ops:
  0.8 2.4 collective-permute-start.1
  9.0 2.2 collective-permute-start.3
  11.2 3.1 %collective-permute-start.2 = (f32[4,146,9]{2,1,0:T(8,128)S(1)}, f32[4,146,9]{2,1,0:T(8,128)S(1)}, u32[]{:S(2)}, u32[]{:S(2)}) collective-permute-start(f32[4,146,9]{2,1,0:T(8,128)S(1)} %get-tuple-element.1120), channel_id=1, source_target_pairs={{0,1},{1,2},{2,3},{4,5},{5,6},{6,7},{8,9},{9,10},{10,11},{12,13},{... | collective-permute-start | bytes 63080 | tf_op jit(solution)/shard_map/ppermute | solution.py:19
  31.5 6.2 %collective-permute-start.5 = (f32[1,146,146]{2,1,0:T(8,128)S(1)}, f32[1,146,146]{2,1,0:T(8,128)S(1)}, u32[]{:S(2)}, u32[]{:S(2)}) collective-permute-start(f32[1,146,146]{2,1,0:T(8,128)S(1)} %get-tuple-element.1118), channel_id=1, source_target_pairs={{0,16},{16,32},{32,48},{48,64},{64,80},{80,96},{96,112},{112,128},... | collective-permute-start | bytes 255800 | tf_op jit(solution)/shard_map/ppermute | solution.py:19
  39.9 4.4 %collective-permute-done.4 = f32[1,146,146]{2,1,0:T(8,128)S(1)} collective-permute-done((f32[1,146,146]{2,1,0:T(8,128)S(1)}, f32[1,146,146]{2,1,0:T(8,128)S(1)}, u32[]{:S(2)}, u32[]{:S(2)}) %collective-permute-start.4) | collective-permute-done | bytes 85296 | tf_op jit(solution)/shard_map/ppermute | solution.py:21
  45.4 2.4 fusion.19
  47.8 31.7 %while.70 = (s32[]{:T(128)}, f32[3,128,128]{2,1,0:T(8,128)S(1)}, f32[128,128]{1,0:T(8,128)S(1)}, f32[3,1,1]{0,2,1:T(1,128)S(1)}, f32[3,1,1]{0,2,1:T(1,128)S(1)},...) while((s32[]{:T(128)}, f32[3,128,128]{2,1,0:T(8,128)S(1)}, ...), condition=%wide.region_8.9_spmd.clone, body=%wide.region_7.8_spmd.clone.sunk | while | flops 753678 | bytes 1442253 | solution.py:74
  53.6 2.0 fusion.65
  61.5 2.0 fusion.65
  69.4 2.0 fusion.65
  77.3 2.0 fusion.65
  79.5 31.0 %while.69 = (s32[]{:T(128)}, f32[3,128,128]{2,1,0:T(8,128)S(1)}, f32[128,128]{1,0:T(8,128)S(1)}, f32[3,1,1]{0,2,1:T(1,128)S(1)}, f32[3,1,1]{0,2,1:T(1,128)S(1)},...) while((s32[]{:T(128)}, f32[3,128,128]{2,1,0:T(8,128)S(1)}, ...), condition=%wide.region_6.7_spmd.clone, body=%wide.region_5.6_spmd.clone.sunk | while | flops 753678 | bytes 1442253 | solution.py:74
  110.5 31.0 %while.68 = (s32[]{:T(128)}, f32[3,128,128]{2,1,0:T(8,128)S(1)}, f32[128,128]{1,0:T(8,128)S(1)}, f32[3,1,1]{0,2,1:T(1,128)S(1)}, f32[3,1,1]{0,2,1:T(1,128)S(1)},...) while((s32[]{:T(128)}, f32[3,128,128]{2,1,0:T(8,128)S(1)}, ...), condition=%wide.region_4.5_spmd.clone, body=%wide.region_3.4_spmd.clone.sunk | while | flops 753678 | bytes 1442253 | solution.py:74
  141.4 24.5 %while.67 = (s32[]{:T(128)}, f32[3,128,128]{2,1,0:T(8,128)S(1)}, f32[128,128]{1,0:T(8,128)S(1)}, f32[3,1,1]{0,2,1:T(1,128)S(1)}, f32[3,1,1]{0,2,1:T(1,128)S(1)},...) while((s32[]{:T(128)}, f32[3,128,128]{2,1,0:T(8,128)S(1)}, ...), condition=%wide.region_2.3_spmd.clone, body=%wide.region_1.2_spmd.clone.sunk | while | flops 753678 | bytes 1442245 | solution.py:74
  166.1 3.1 %dynamic_update_slice.19 = f32[1,4,160,160]{3,2,1,0:T(8,128)S(1)} dynamic-update-slice(f32[1,4,160,160]{3,2,1,0:T(8,128)S(1)} %broadcast_in_dim.30.clone, f32[1,4,128,128]{3,2,1,0:T(8,128)S(1)} %maximum_bitcast_fusion.3, s32[]{:T(128)} %constant.961.clone.1, s32[]{:T(128)} %constant.961.clone.1, s32[]{:T(128)S(6)} %select_n.135, s32[]{:T(128)S(6)} %select_n.136) | dynamic-update-slice | bytes 524292 | tf_op jit(solution)/shard_map/dynamic_update_slice | solution.py:103
  169.2 3.1 %dynamic_update_slice.18 = f32[1,4,160,160]{3,2,1,0:T(8,128)S(1)} dynamic-update-slice(f32[1,4,160,160]{3,2,1,0:T(8,128)S(1)} %broadcast_in_dim.30.clone.1, f32[1,4,128,128]{3,2,1,0:T(8,128)S(1)} %maximum_bitcast_fusion.2, s32[]{:T(128)} %constant.961.clone.1, s32[]{:T(128)} %constant.961.clone.1, s32[]{:T(128)S(6)} %select_n.133, s32[]{:T(128)S(6)} %select_n.134) | dynamic-update-slice | bytes 524292 | tf_op jit(solution)/shard_map/dynamic_update_slice | solution.py:103
  172.4 3.1 %dynamic_update_slice.17 = f32[1,4,160,160]{3,2,1,0:T(8,128)S(1)} dynamic-update-slice(f32[1,4,160,160]{3,2,1,0:T(8,128)S(1)} %broadcast_in_dim.30.clone.2, f32[1,4,128,128]{3,2,1,0:T(8,128)S(1)} %maximum_bitcast_fusion.1, s32[]{:T(128)} %constant.961.clone.1, s32[]{:T(128)} %constant.961.clone.1, s32[]{:T(128)S(6)} %select_n.131, s32[]{:T(128)S(6)} %select_n.132) | dynamic-update-slice | bytes 524292 | tf_op jit(solution)/shard_map/dynamic_update_slice | solution.py:103
  175.5 3.1 %dynamic_update_slice.16 = f32[1,4,160,160]{3,2,1,0:T(8,128)S(1)} dynamic-update-slice(f32[1,4,160,160]{3,2,1,0:T(8,128)S(1)} %broadcast_in_dim.30.clone.3, f32[1,4,128,128]{3,2,1,0:T(8,128)S(1)} %maximum_bitcast_fusion, s32[]{:T(128)} %constant.961.clone.1, s32[]{:T(128)} %constant.961.clone.1, s32[]{:T(128)S(6)} %select_n.129, s32[]{:T(128)S(6)} %select_n.130) | dynamic-update-slice | bytes 524292 | tf_op jit(solution)/shard_map/dynamic_update_slice | solution.py:103
  183.0 3.1 %collective-permute-start.7 = (f32[4,4,128,32]{2,3,1,0:T(8,128)S(1)}, f32[4,4,128,32]{2,3,1,0:T(8,128)S(1)}, u32[]{:S(2)}, u32[]{:S(2)}) collective-permute-start(f32[4,4,128,32]{2,3,1,0:T(8,128)S(1)} %copy.32), channel_id=1, source_target_pairs={{0,1},{1,2},{2,3},{4,5},{5,6},{6,7},{8,9},{9,10},{10,11},{12,13},{... | collective-permute-start | bytes 786440 | tf_op jit(solution)/shard_map/ppermute | solution.py:31
  188.1 2.3 slice.439
  194.0 6.2 %collective-permute-done.6 = f32[4,4,32,128]{3,2,1,0:T(8,128)S(1)} collective-permute-done((f32[4,4,32,128]{3,2,1,0:T(8,128)}, f32[4,4,32,128]{3,2,1,0:T(8,128)S(1)}, u32[]{:S(2)}, u32[]{:S(2)}) %collective-permute-start.6) | collective-permute-done | bytes 262176 | tf_op jit(solution)/shard_map/ppermute | solution.py:31
  202.5 2.0 scatter-add.11
  208.2 17.6 %all-to-all-start = ((f32[1,4,4,128,128]{4,2,1,0,3:T(4,128)}), f32[1,4,4,128,128]{4,2,1,0,3:T(4,128)S(1)}, u32[]{:S(2)}, u32[]{:S(2)}) async-start(f32[1,4,4,128,128]{4,2,1,0,3:T(4,128)} %copy.34), calls=%async_computation | async-start | bytes 2097152 | tf_op jit(solution)/shard_map/all_to_all | solution.py:116
  225.9 55.6 %all-to-all-done = f32[1,4,4,128,128]{4,2,1,0,3:T(4,128)S(1)} async-done(((f32[1,4,4,128,128]{4,2,1,0,3:T(4,128)}), f32[1,4,4,128,128]{4,2,1,0,3:T(4,128)S(1)}, u32[]{:S(2)}, u32[]{:S(2)}) %all-to-all-start) | async-done | bytes 1048608 | tf_op jit(solution)/shard_map/all_to_all | solution.py:116
  (218 shorter events, 100.7 us)
Async XLA Ops:
  0.0 6.8 %copy-start = (s32[4,32,2]{1,2,0:T(2,128)S(1)}, s32[4,32,2]{1,2,0:T(2,128)}, u32[]{:S(2)}) copy-start(s32[4,32,2]{1,2,0:T(2,128)} %param.26) | copy-start | bytes 3076
  0.0 44.3 %copy-start.3 = (f32[4,128,128]{2,1,0:T(8,128)S(1)}, f32[4,128,128]{2,1,0:T(8,128)}, u32[]{:S(2)}) copy-start(f32[4,128,128]{2,1,0:T(8,128)} %param.21) | copy-start | bytes 786436
  0.0 39.6 %copy-start.9 = (s32[4,128,2]{1,2,0:T(2,128)S(1)}, s32[4,128,2]{1,2,0:T(2,128)}, u32[]{:S(2)}) copy-start(s32[4,128,2]{1,2,0:T(2,128)} %param.25) | copy-start | bytes 12292
  0.8 6.2 %collective-permute-start.1 = (f32[4,9,128]{2,1,0:T(8,128)S(1)}, f32[4,9,128]{2,1,0:T(8,128)S(1)}, u32[]{:S(2)}, u32[]{:S(2)}) collective-permute-start(f32[4,9,128]{2,1,0:T(8,128)S(1)} %get-tuple-element.1123), channel_id=1, source_target_pairs={{4,0},{8,4},{12,8},{5,1},{9,5},{13,9},{6,2},{10,6},{14,10},{7,3},{... | collective-permute-start | bytes 55304 | tf_op jit(solution)/shard_map/ppermute | solution.py:21
  3.2 4.7 %collective-permute-start = (f32[4,9,128]{2,1,0:T(8,128)S(1)}, f32[4,9,128]{2,1,0:T(8,128)S(1)}, u32[]{:S(2)}, u32[]{:S(2)}) collective-permute-start(f32[4,9,128]{2,1,0:T(8,128)S(1)} %get-tuple-element.1122), channel_id=1, source_target_pairs={{0,4},{4,8},{8,12},{1,5},{5,9},{9,13},{2,6},{6,10},{10,14},{3,7},{... | collective-permute-start | bytes 55304 | tf_op jit(solution)/shard_map/ppermute | solution.py:19
  9.0 20.9 %collective-permute-start.3 = (f32[4,146,9]{2,1,0:T(8,128)S(1)}, f32[4,146,9]{2,1,0:T(8,128)S(1)}, u32[]{:S(2)}, u32[]{:S(2)}) collective-permute-start(f32[4,146,9]{2,1,0:T(8,128)S(1)} %get-tuple-element.1121), channel_id=1, source_target_pairs={{1,0},{2,1},{3,2},{5,4},{6,5},{7,6},{9,8},{10,9},{11,10},{13,12},{... | collective-permute-start | bytes 63080 | tf_op jit(solution)/shard_map/ppermute | solution.py:21
  11.2 18.8 %collective-permute-start.2 = (f32[4,146,9]{2,1,0:T(8,128)S(1)}, f32[4,146,9]{2,1,0:T(8,128)S(1)}, u32[]{:S(2)}, u32[]{:S(2)}) collective-permute-start(f32[4,146,9]{2,1,0:T(8,128)S(1)} %get-tuple-element.1120), channel_id=1, source_target_pairs={{0,1},{1,2},{2,3},{4,5},{5,6},{6,7},{8,9},{9,10},{10,11},{12,13},{... | collective-permute-start | bytes 63080 | tf_op jit(solution)/shard_map/ppermute | solution.py:19
  29.9 15.4 %copy-start.6 = (f32[4,146,9]{2,1,0:T(8,128)}, f32[4,146,9]{2,1,0:T(8,128)S(1)}, u32[]{:S(2)}) copy-start(f32[4,146,9]{2,1,0:T(8,128)S(1)} %collective-permute-done.3) | copy-start | bytes 63076
  29.9 15.4 %copy-start.7 = (f32[4,146,9]{2,1,0:T(8,128)}, f32[4,146,9]{2,1,0:T(8,128)S(1)}, u32[]{:S(2)}) copy-start(f32[4,146,9]{2,1,0:T(8,128)S(1)} %collective-permute-done.2) | copy-start | bytes 63076
  31.4 14.0 %copy-start.4 = (f32[4,128,128]{2,1,0:T(8,128)S(1)}, f32[4,128,128]{2,1,0:T(8,128)}, u32[]{:S(2)}) copy-start(f32[4,128,128]{2,1,0:T(8,128)} %param.21) | copy-start | bytes 786436
  31.5 8.4 %collective-permute-start.5 = (f32[1,146,146]{2,1,0:T(8,128)S(1)}, f32[1,146,146]{2,1,0:T(8,128)S(1)}, u32[]{:S(2)}, u32[]{:S(2)}) collective-permute-start(f32[1,146,146]{2,1,0:T(8,128)S(1)} %get-tuple-element.1118), channel_id=1, source_target_pairs={{0,16},{16,32},{32,48},{48,64},{64,80},{80,96},{96,112},{112,128},... | collective-permute-start | bytes 255800 | tf_op jit(solution)/shard_map/ppermute | solution.py:19
  37.7 6.5 %collective-permute-start.4 = (f32[1,146,146]{2,1,0:T(8,128)S(1)}, f32[1,146,146]{2,1,0:T(8,128)S(1)}, u32[]{:S(2)}, u32[]{:S(2)}) collective-permute-start(f32[1,146,146]{2,1,0:T(8,128)S(1)} %get-tuple-element.1117), channel_id=1, source_target_pairs={{16,0},{32,16},{48,32},{64,48},{80,64},{96,80},{112,96},{128,112},... | collective-permute-start | bytes 255800 | tf_op jit(solution)/shard_map/ppermute | solution.py:21
  45.4 2.4 copy-start.8
  178.9 1.5 copy-start.2
  183.0 9.7 %collective-permute-start.7 = (f32[4,4,128,32]{2,3,1,0:T(8,128)S(1)}, f32[4,4,128,32]{2,3,1,0:T(8,128)S(1)}, u32[]{:S(2)}, u32[]{:S(2)}) collective-permute-start(f32[4,4,128,32]{2,3,1,0:T(8,128)S(1)} %copy.32), channel_id=1, source_target_pairs={{0,1},{1,2},{2,3},{4,5},{5,6},{6,7},{8,9},{9,10},{10,11},{12,13},{... | collective-permute-start | bytes 786440 | tf_op jit(solution)/shard_map/ppermute | solution.py:31
  186.8 13.4 %collective-permute-start.6 = (f32[4,4,32,128]{3,2,1,0:T(8,128)}, f32[4,4,32,128]{3,2,1,0:T(8,128)S(1)}, u32[]{:S(2)}, u32[]{:S(2)}) collective-permute-start(f32[4,4,32,128]{3,2,1,0:T(8,128)} %pad_maximum_fusion.14), channel_id=1, source_target_pairs={{0,4},{4,8},{8,12},{1,5},{5,9},{9,13},{2,6},{6,10},{10,14},{3,7},{... | collective-permute-start | bytes 786440 | tf_op jit(solution)/shard_map/ppermute | solution.py:31
  191.2 13.3 %collective-permute-start.8 = (f32[4,4,32,32]{3,2,1,0:T(8,128)}, f32[4,4,32,32]{3,2,1,0:T(8,128)}, u32[]{:S(2)}, u32[]{:S(2)}) collective-permute-start(f32[4,4,32,32]{3,2,1,0:T(8,128)} %pad_maximum_fusion.13), channel_id=1, source_target_pairs={{0,5},{1,6},{2,7},{3,8},{4,9},{5,10},{6,11},{7,12},{8,13},{9,14},{... | collective-permute-start | bytes 196616 | tf_op jit(solution)/shard_map/ppermute | solution.py:31
  194.0 6.9 %copy-start.5 = (f32[4,4,128,32]{3,2,1,0:T(8,128)S(1)}, f32[4,4,128,32]{3,2,1,0:T(8,128)}, u32[]{:S(2)}) copy-start(f32[4,4,128,32]{3,2,1,0:T(8,128)} %copy.33) | copy-start | bytes 786436
  200.9 1.5 copy-start.1
  204.5 21.3 %copy-start.10 = (s32[4,32]{1,0:T(4,128)S(1)}, s32[4,32]{1,0:T(4,128)}, u32[]{:S(2)}) copy-start(s32[4,32]{1,0:T(4,128)} %param.27) | copy-start | bytes 1540
  208.2 73.3 %all-to-all-start = ((f32[1,4,4,128,128]{4,2,1,0,3:T(4,128)}), f32[1,4,4,128,128]{4,2,1,0,3:T(4,128)S(1)}, u32[]{:S(2)}, u32[]{:S(2)}) async-start(f32[1,4,4,128,128]{4,2,1,0,3:T(4,128)} %copy.34), calls=%async_computation | async-start | bytes 2097152 | tf_op jit(solution)/shard_map/all_to_all | solution.py:116
where the time goes:
time: 285 us; the launch traced here: 283 us
  waiting for transfers between devices  67.2 us (24%)
  other arithmetic  64.2 us (23%)
  local copies, waits for them, and re-layouts  56.2 us (20%)
  starting transfers between devices  40.5 us (14%)
  loops' own time  39.5 us (14%)
  between operations  15.4 us (5%)
    all_to_all x1, waiting for transfers between devices, on_device(): lax.all_to_all(own_tile[None], 'gz', split_axis=3, concat_axis=0, tiled=T...  55.6 us
    another operation x4, loops' own time, render_layers(): lax.scan(advance, start_carry, (inner, normals[0], normals[1], normals[2]...  39.5 us
    mul x16, other arithmetic, advance(): hues = jax.nn.sigmoid(offsets + slopes * value[None]) * shade[None]  31.1 us
    all_to_all x1, starting transfers between devices, on_device(): lax.all_to_all(own_tile[None], 'gz', split_axis=3, concat_axis=0, tiled=T...  17.6 us
    dynamic_update_slice x4, local copies, waits for them, and re-layouts, on_device(): lax.dynamic_update_slice(blank, layers[view], (zero, moved[view, 0], move...  12.3 us
    add x32, other arithmetic, advance(): return ((color + hues * weight[None], depth + density), None)  11.8 us
    ppermute x3, starting transfers between devices, padded(): lax.ppermute(tail, axis, [(i, (i + 1) % count) for i in range(ends)])  10.6 us
    slice x16, local copies, waits for them, and re-layouts, advance(): towards[view, 0]  9.97 us
  transfers between devices with their start and end apart: 10, of which 5 were waited for; matrix products, arithmetic and copies ran while one was open for 4% of the time, Pallas kernels for 0%

commit v1 on v0

v1 whole, which is shorter than its diff:
```python
import functools

import jax
import jax.numpy as jnp
from jax import lax
from jax.experimental import pallas as pl
from jax.experimental.pallas import tpu as pltpu
from jax.sharding import PartitionSpec as P

VIEWS = 4
BZ = 4
TILE = 128
HALO = 40
EXT = HALO + TILE
BASE = 8
CHUNK = 16

VMEM = pl.BlockSpec(memory_space=pltpu.VMEM)
SMEM = pl.BlockSpec(memory_space=pltpu.SMEM)


def render_kernel(
    moves_ref, light_ref, palette_ref, rate_ref,
    own_ref, above_ref, left_ref, corner_ref, front_ref, back_ref, below_ref, right_ref,
    out_ref,
    core_s, side_s, near_s, fields,
):
    gy = lax.axis_index("gy")
    gx = lax.axis_index("gx")
    lane8 = lax.broadcasted_iota(jnp.int32, (8, TILE), 1)

    for k in range(BZ):
        core_s[k, BASE : BASE + HALO] = above_ref[k]
        core_s[k, BASE + HALO : BASE + EXT] = own_ref[k]
        core_s[k, BASE + EXT : BASE + EXT + 1] = below_ref[k : k + 1]
        pack = 0 if k in (0, 3) else 1
        corner, left, below = corner_ref[pack], left_ref[pack], below_ref[4 + pack : 5 + pack]
        if k >= 2:
            corner = pltpu.roll(corner, 64, axis=1)
            left = pltpu.roll(left, 64, axis=1)
            below = pltpu.roll(jnp.broadcast_to(below, (8, TILE)), 64, axis=1)[0:1]
        side_s[k, BASE : BASE + HALO] = corner
        side_s[k, BASE + HALO : BASE + EXT] = left
        side_s[k, BASE + EXT : BASE + EXT + 1] = below
    near_s[0] = pltpu.roll(front_ref[1], 64, axis=1)
    near_s[1] = back_ref[1]

    def derive(i, carry):
        row = pl.multiple_of(i * 8, 8)
        at = pl.multiple_of(row + BASE, 8)
        core = [core_s[k, pl.ds(at, 8)] for k in range(BZ)]
        side = [side_s[k, pl.ds(at, 8)] for k in range(BZ)]
        front = (front_ref[0, pl.ds(row, 8)], near_s[0, pl.ds(row, 8)])
        back = (back_ref[0, pl.ds(row, 8)], near_s[1, pl.ds(row, 8)])
        edge = right_ref[pl.ds(row, 8)]
        for k in range(BZ):
            c, s = core[k], side[k]
            c_next = pltpu.roll(c, TILE - 1, axis=1)
            s_prev = pltpu.roll(s, 1, axis=1)
            c_right = jnp.where(
                lane8 == TILE - 1, pltpu.roll(edge, TILE - 1 - 32 * k, axis=1), c_next
            )
            c_left = jnp.where(lane8 == 0, s_prev, pltpu.roll(c, 1, axis=1))
            s_right = jnp.where(lane8 == TILE - 1, c_next, pltpu.roll(s, TILE - 1, axis=1))
            for half, (value, xr, xl, ref, before, after) in enumerate(
                (
                    (c, c_right, c_left, core_s,
                     front[0] if k == 0 else core[k - 1], back[0] if k == 3 else core[k + 1]),
                    (s, s_right, s_prev, side_s,
                     front[1] if k == 0 else side[k - 1], back[1] if k == 3 else side[k + 1]),
                )
            ):
                gd = 0.5 * (after - before)
                gr = 0.5 * (ref[k, pl.ds(at + 1, 8)] - ref[k, pl.ds(at - 1, 8)])
                gc = 0.5 * (xr - xl)
                factor = lax.rsqrt(gd * gd + gr * gr + gc * gc + 1.0)
                fields[0, k, half, pl.ds(row, 8)] = jnp.tanh(value)
                fields[1, k, half, pl.ds(row, 8)] = gd * factor
                fields[2, k, half, pl.ds(row, 8)] = gr * factor
                fields[3, k, half, pl.ds(row, 8)] = gc * factor
                for c3 in range(3):
                    arg = palette_ref[c3, 0] + palette_ref[c3, 1] * value
                    fields[4 + c3, k, half, pl.ds(row, 8)] = 0.5 + 0.5 * jnp.tanh(0.5 * arg)
        return carry

    lax.fori_loop(0, EXT // 8, derive, 0)

    lane = lax.broadcasted_iota(jnp.int32, (CHUNK, TILE), 1)
    rows = lax.broadcasted_iota(jnp.int32, (CHUNK, TILE), 0)
    for view in range(VIEWS):
        ld = jnp.full((8, TILE), light_ref[view, 0], jnp.float32)
        lr = jnp.full((8, TILE), light_ref[view, 1], jnp.float32)
        lc = jnp.full((8, TILE), light_ref[view, 2], jnp.float32)
        length = jnp.sqrt(ld * ld + lr * lr + lc * lc + 1.0)
        td, tr, tc = ((v / length)[0:1] for v in (ld, lr, lc))
        rate = rate_ref[view]
        off_r, off_c = moves_ref[view * 10 + 8], moves_ref[view * 10 + 9]

        def shade_rows(j, carry, view=view, td=td, tr=tr, tc=tc, rate=rate, off_r=off_r, off_c=off_c):
            base = pl.multiple_of(j * CHUNK, CHUNK)
            inside = jnp.logical_and(
                rows + (gy * TILE + base) >= off_r, lane + gx * TILE >= off_c
            )
            depth = jnp.zeros((CHUNK, TILE), jnp.float32)
            clear = jnp.ones((CHUNK, TILE), jnp.float32)
            color = [jnp.zeros((CHUNK, TILE), jnp.float32) for _ in range(3)]
            for k in range(BZ):
                dy = moves_ref[view * 10 + 2 * k]
                dx = moves_ref[view * 10 + 2 * k + 1]
                start = base + (HALO - dy)
                own = lane < TILE - dx

                def sample(a):
                    core = fields[a, k, 0, pl.ds(start, CHUNK)]
                    side = fields[a, k, 1, pl.ds(start, CHUNK)]
                    return pltpu.roll(jnp.where(own, core, side), dx, axis=1)

                density = rate * (1.0 + sample(0))
                dot = sample(1) * td + sample(2) * tr + sample(3) * tc
                kept = clear * jnp.exp(-density)
                weight = (0.25 + 0.75 * dot * dot) * (clear - kept)
                for c3 in range(3):
                    color[c3] = color[c3] + sample(4 + c3) * weight
                depth = depth + density
                clear = kept
            for c4, value in enumerate(color + [depth]):
                value = jnp.where(inside, value, 0.0)
                for q in range(CHUNK // 4):
                    out_ref[j * (CHUNK // 4) + q, c4 * 16 + view * 4 : c4 * 16 + view * 4 + 4] = (
                        value[4 * q : 4 * q + 4]
                    )
            return carry

        lax.fori_loop(0, TILE // CHUNK, shade_rows, 0)


def composite_kernel(order_ref, pieces_ref, out_ref):
    bricks = pieces_ref.shape[0]
    for view in range(VIEWS):
        cover = jnp.zeros((4, TILE), jnp.float32)
        color = [jnp.zeros((4, TILE), jnp.float32) for _ in range(3)]
        for place in range(bricks):
            brick = order_ref[view, place]
            clear = jnp.exp(-cover)
            for c3 in range(3):
                at = c3 * 16 + view * 4
                color[c3] = color[c3] + pieces_ref[brick, at : at + 4] * clear
            at = 48 + view * 4
            cover = cover + pieces_ref[brick, at : at + 4]
        for c3 in range(3):
            out_ref[view, c3, 0] = color[c3]
        out_ref[view, 3, 0] = 1.0 - jnp.exp(-cover)


def moved(value, axes, steps):
    count = lax.axis_size(axes)
    first, last = max(0, -steps), min(count, count - steps)
    return lax.ppermute(value, axes, [(i, i + steps) for i in range(first, last)])


def diagonal(value):
    n_y, n_x = lax.axis_size("gy"), lax.axis_size("gx")
    pairs = [
        (y * n_x + x, (y + 1) * n_x + x + 1) for y in range(n_y - 1) for x in range(n_x - 1)
    ]
    return lax.ppermute(value, ("gy", "gx"), pairs)


def on_device(pressure, light, palette, rate, shear, offset, order):
    bricks = order.shape[1]
    brick = lax.axis_index("gz")
    zero = jnp.zeros((), jnp.int32)

    shifts = lax.dynamic_slice(shear, (zero, brick * BZ, zero), (VIEWS, BZ, 2))
    place = lax.dynamic_slice(offset, (zero, brick, zero), (VIEWS, 1, 2))
    moves = jnp.concatenate([shifts + place, place], axis=1).reshape(-1)

    half = TILE // 2
    pack = jnp.concatenate(
        [
            jnp.stack([pressure[3, :, half:], pressure[2, :, half:]]),
            jnp.stack([pressure[0, :, half:], pressure[1, :, half:]]),
        ],
        axis=2,
    )
    above = moved(pressure[:, TILE - HALO :], "gy", 1)
    left = moved(pack, "gx", 1)
    corner = diagonal(pack[:, TILE - HALO :])

    def slice_with_margins(k):
        return jnp.stack(
            [
                jnp.concatenate([above[k], pressure[k]], axis=0),
                jnp.concatenate([corner[0], left[0]], axis=0),
            ]
        )

    front = moved(slice_with_margins(3), "gz", 1)
    back = moved(slice_with_margins(0), "gz", -1)
    below = moved(jnp.concatenate([pressure[:, 0], left[:, 0]], axis=0), "gy", -1)
    edge = jnp.concatenate(
        [jnp.concatenate([above[k, :, :32], pressure[k, :, :32]], axis=0) for k in range(BZ)], axis=1
    )
    right = moved(edge, "gx", -1)

    pieces = pl.pallas_call(
        render_kernel,
        out_shape=jax.ShapeDtypeStruct((bricks, 4 * VIEWS * 4, TILE), jnp.float32),
        in_specs=[SMEM] * 4 + [VMEM] * 8,
        out_specs=VMEM,
        scratch_shapes=[
            pltpu.VMEM((BZ, BASE + EXT + 8, TILE), jnp.float32),
            pltpu.VMEM((BZ, BASE + EXT + 8, TILE), jnp.float32),
            pltpu.VMEM((2, EXT, TILE), jnp.float32),
            pltpu.VMEM((7, BZ, 2, EXT, TILE), jnp.float32),
        ],
        compiler_params=pltpu.CompilerParams(vmem_limit_bytes=32 * 1024 * 1024),
        name="render",
    )(moves, light, palette, rate, pressure, above, left, corner, front, back, below, right)

    strips = lax.all_to_all(pieces, "gz", 0, 0, tiled=True)

    return pl.pallas_call(
        composite_kernel,
        out_shape=jax.ShapeDtypeStruct((VIEWS, 4, 1, 4, TILE), jnp.float32),
        in_specs=[SMEM, VMEM],
        out_specs=VMEM,
        compiler_params=pltpu.CompilerParams(vmem_limit_bytes=16 * 1024 * 1024),
        name="composite",
    )(order, strips)


def solution(mesh):
    return jax.shard_map(
        on_device,
        mesh=mesh,
        in_specs=(P("gz", "gy", "gx"), P(), P(), P(), P(), P(), P()),
        out_specs=P(None, None, "gz", "gy", "gx"),
        check_vma=False,
    )
```

time: 285 us -> 108 us (0.38)
  the two profiles are of different devices: /device:TPU:27 before, /device:TPU:3 now
where the time goes in v1:
time: 108 us
  blocking collectives  70.9 us (66%)
  starting transfers between devices  21 us (19%)
  Pallas kernels  8.67 us (8%)
  local copies, waits for them, and re-layouts  3.47 us (3%)
  waiting for transfers between devices  2.65 us (2%)
    all_to_all x1, blocking collectives, on_device(): strips = lax.all_to_all(pieces, 'gz', 0, 0, tiled=True)  70.9 us
    ppermute x6, starting transfers between devices, moved(): lax.ppermute(value, axes, [(i, i + steps) for i in range(first, last)])  16.9 us
    pallas_call x1, Pallas kernels, on_device(): pl.pallas_call(render_kernel, out_shape=jax.ShapeDtypeStruct((bricks, 4 *...  7.29 us
    ppermute x1, starting transfers between devices, diagonal(): return lax.ppermute(value, ('gy', 'gx'), pairs)  4.13 us
    ppermute x6, waiting for transfers between devices, moved(): lax.ppermute(value, axes, [(i, i + steps) for i in range(first, last)])  2.64 us
  transfers between devices with their start and end apart: 7, of which 1 were waited for; matrix products, arithmetic and copies ran while one was open for 2% of the time, Pallas kernels for 0%

profile of v1, /device:TPU:3, one launch (start us, length us, event | category | flops | bytes accessed | tf_op | source)
XLA Modules:
  0.0 107.5 jit_solution(13961795738794336589)
XLA Ops:
  0.0 1.0 slice.65
  1.0 3.2 %collective-permute-start = (f32[4,40,128]{2,1,0:T(8,128)S(1)}, f32[4,40,128]{2,1,0:T(8,128)S(1)}, u32[]{:S(2)}, u32[]{:S(2)}) collective-permute-start(f32[4,40,128]{2,1,0:T(8,128)S(1)} %slice.65), channel_id=1, source_target_pairs={{0,4},{4,8},{8,12},{1,5},{5,9},{9,13},{2,6},{6,10},{10,14},{3,7},{... | collective-permute-start | bytes 245768 | tf_op jit(solution)/shard_map/ppermute | solution.py:158
  4.2 1.0 stack.23
  5.2 0.1 fusion
  5.3 0.1 pad_maximum_fusion.2
  5.4 4.1 %collective-permute-start.2 = (f32[2,40,128]{2,1,0:T(8,128)S(1)}, f32[2,40,128]{2,1,0:T(8,128)S(1)}, u32[]{:S(2)}, u32[]{:S(2)}) collective-permute-start(f32[2,40,128]{2,1,0:T(8,128)S(1)} %slice.85), channel_id=1, source_target_pairs={{0,5},{1,6},{2,7},{4,9},{5,10},{6,11},{8,13},{9,14},{10,15},{16,21... | collective-permute-start | bytes 122888 | tf_op jit(solution)/shard_map/ppermute | solution.py:166
  9.5 0.1 copy.44
  9.7 2.8 %collective-permute-start.1 = (f32[2,128,128]{2,0,1:T(2,128)S(1)}, f32[2,128,128]{2,0,1:T(2,128)S(1)}, u32[]{:S(2)}, u32[]{:S(2)}) collective-permute-start(f32[2,128,128]{2,0,1:T(2,128)S(1)} %copy.44), channel_id=1, source_target_pairs={{0,1},{1,2},{2,3},{4,5},{5,6},{6,7},{8,9},{9,10},{10,11},{12,13},{... | collective-permute-start | bytes 393224 | tf_op jit(solution)/shard_map/ppermute | solution.py:158
  12.6 0.1 constant_dynamic-slice_fusion
  12.6 0.1 copy.41
  12.7 0.1 copy.42
  12.8 0.6 copy-done.5
  13.6 0.1 maximum_maximum_fusion
  13.7 2.5 %collective-permute-start.6 = (f32[168,128]{1,0:T(8,128)S(1)}, f32[168,128]{1,0:T(8,128)S(1)}, u32[]{:S(2)}, u32[]{:S(2)}) collective-permute-start(f32[168,128]{1,0:T(8,128)S(1)} %maximum_maximum_fusion), channel_id=1, source_target_pairs={{1,0},{2,1},{3,2},{5,4},{6,5},{7,6},{9,8},{10,9},{11,10},{13,12},{... | collective-permute-start | bytes 258056 | tf_op jit(solution)/shard_map/ppermute | solution.py:158
  16.3 3.7 %collective-permute-start.4 = (f32[2,168,128]{2,1,0:T(8,128)S(1)}, f32[2,168,128]{2,1,0:T(8,128)S(1)}, u32[]{:S(2)}, u32[]{:S(2)}) collective-permute-start(f32[2,168,128]{2,1,0:T(8,128)S(1)} %get-tuple-element.13), channel_id=1, source_target_pairs={{16,0},{32,16},{48,32},{64,48},{80,64},{96,80},{112,96},{128,112},... | collective-permute-start | bytes 516104 | tf_op jit(solution)/shard_map/ppermute | solution.py:158
  20.0 3.4 %collective-permute-start.3 = (f32[2,168,128]{2,1,0:T(8,128)S(1)}, f32[2,168,128]{2,1,0:T(8,128)S(1)}, u32[]{:S(2)}, u32[]{:S(2)}) collective-permute-start(f32[2,168,128]{2,1,0:T(8,128)S(1)} %get-tuple-element.14), channel_id=1, source_target_pairs={{0,16},{16,32},{32,48},{48,64},{64,80},{80,96},{96,112},{112,128},... | collective-permute-start | bytes 516104 | tf_op jit(solution)/shard_map/ppermute | solution.py:158
  23.5 1.3 %collective-permute-start.5 = (f32[6,128]{1,0:T(8,128)S(1)}, f32[6,128]{1,0:T(8,128)S(1)}, u32[]{:S(2)}, u32[]{:S(2)}) collective-permute-start(f32[6,128]{1,0:T(8,128)S(1)} %pad_maximum_fusion.3), channel_id=1, source_target_pairs={{4,0},{8,4},{12,8},{5,1},{9,5},{13,9},{6,2},{10,6},{14,10},{7,3},{... | collective-permute-start | bytes 9224 | tf_op jit(solution)/shard_map/ppermute | solution.py:158
  24.9 0.1 copy.46.palette_ref
  25.0 0.1 copy.43
  25.1 0.1 reshape.3.moves_ref
  25.2 2.6 %collective-permute-done.5.below_ref = f32[6,128]{1,0:T(8,128)S(1)} collective-permute-done((f32[6,128]{1,0:T(8,128)S(1)}, f32[6,128]{1,0:T(8,128)S(1)}, u32[]{:S(2)}, u32[]{:S(2)}) %collective-permute-start.5) | collective-permute-done | bytes 3104 | tf_op jit(solution)/shard_map/ppermute | solution.py:158
  27.9 7.3 %render.1 = f32[32,64,128]{2,1,0:T(8,128)S(1)} custom-call(s32[40]{0:T(128)S(1)} %reshape.3.moves_ref, f32[4,3]{1,0:T(4,128)S(1)} %copy-done.2, f32[3,2]{1,0:T(4,128)S(1)} %copy.46.palette_ref, f32[4]{0:T(128)S(1)} %copy-done.4, f32[4,128,128]{2,1,0:T(8,128)S(1)} %copy-done.1, f32[4,40,128]{2,1,0:T(8,128)S(1)} %collective-permute-done.above_ref, ...), custom_call_target="tpu_custom_call" | custom-call | tf_op jit(solution)/shard_map/render/pallas_call | solution.py:206
  35.2 70.9 %all_to_all.5.pieces_ref = f32[32,64,128]{2,1,0:T(8,128)S(1)} all-to-all(f32[32,64,128]{2,1,0:T(8,128)S(1)} %render.1), channel_id=1, replica_groups=mesh['gz'=32,'gy'=4,'gx'=4] {'gz'}, dimensions={0} | all-to-all | bytes 2097152 | tf_op jit(solution)/shard_map/all_to_all | solution.py:221
  106.1 1.4 %composite.1 = f32[4,4,1,4,128]{4,3,2,1,0:T(4,128)} custom-call(s32[4,32]{1,0:T(4,128)S(1)} %copy-done.3, f32[32,64,128]{2,1,0:T(8,128)S(1)} %all_to_all.5.pieces_ref), custom_call_target="tpu_custom_call" | custom-call | tf_op jit(solution)/shard_map/composite/pallas_call | solution.py:223
  (35 shorter events, 0.4 us)
Async XLA Ops:
  0.0 12.5 %copy-start = (s32[4,32,2]{1,2,0:T(2,128)S(1)}, s32[4,32,2]{1,2,0:T(2,128)}, u32[]{:S(2)}) copy-start(s32[4,32,2]{1,2,0:T(2,128)} %param.12) | copy-start | bytes 3076
  0.0 5.2 %copy-start.1 = (f32[4,128,128]{2,1,0:T(8,128)S(1)}, f32[4,128,128]{2,1,0:T(8,128)}, u32[]{:S(2)}) copy-start(f32[4,128,128]{2,1,0:T(8,128)} %own_ref.1) | copy-start | bytes 786436
  1.0 12.6 %collective-permute-start = (f32[4,40,128]{2,1,0:T(8,128)S(1)}, f32[4,40,128]{2,1,0:T(8,128)S(1)}, u32[]{:S(2)}, u32[]{:S(2)}) collective-permute-start(f32[4,40,128]{2,1,0:T(8,128)S(1)} %slice.65), channel_id=1, source_target_pairs={{0,4},{4,8},{8,12},{1,5},{5,9},{9,13},{2,6},{6,10},{10,14},{3,7},{... | collective-permute-start | bytes 245768 | tf_op jit(solution)/shard_map/ppermute | solution.py:158
  5.4 8.1 %collective-permute-start.2 = (f32[2,40,128]{2,1,0:T(8,128)S(1)}, f32[2,40,128]{2,1,0:T(8,128)S(1)}, u32[]{:S(2)}, u32[]{:S(2)}) collective-permute-start(f32[2,40,128]{2,1,0:T(8,128)S(1)} %slice.85), channel_id=1, source_target_pairs={{0,5},{1,6},{2,7},{4,9},{5,10},{6,11},{8,13},{9,14},{10,15},{16,21... | collective-permute-start | bytes 122888 | tf_op jit(solution)/shard_map/ppermute | solution.py:166
  9.7 6.5 %collective-permute-start.1 = (f32[2,128,128]{2,0,1:T(2,128)S(1)}, f32[2,128,128]{2,0,1:T(2,128)S(1)}, u32[]{:S(2)}, u32[]{:S(2)}) collective-permute-start(f32[2,128,128]{2,0,1:T(2,128)S(1)} %copy.44), channel_id=1, source_target_pairs={{0,1},{1,2},{2,3},{4,5},{5,6},{6,7},{8,9},{9,10},{10,11},{12,13},{... | collective-permute-start | bytes 393224 | tf_op jit(solution)/shard_map/ppermute | solution.py:158
  12.7 0.7 copy-start.5
  13.7 14.2 %collective-permute-start.6 = (f32[168,128]{1,0:T(8,128)S(1)}, f32[168,128]{1,0:T(8,128)S(1)}, u32[]{:S(2)}, u32[]{:S(2)}) collective-permute-start(f32[168,128]{1,0:T(8,128)S(1)} %maximum_maximum_fusion), channel_id=1, source_target_pairs={{1,0},{2,1},{3,2},{5,4},{6,5},{7,6},{9,8},{10,9},{11,10},{13,12},{... | collective-permute-start | bytes 258056 | tf_op jit(solution)/shard_map/ppermute | solution.py:158
  16.3 11.6 %collective-permute-start.4 = (f32[2,168,128]{2,1,0:T(8,128)S(1)}, f32[2,168,128]{2,1,0:T(8,128)S(1)}, u32[]{:S(2)}, u32[]{:S(2)}) collective-permute-start(f32[2,168,128]{2,1,0:T(8,128)S(1)} %get-tuple-element.13), channel_id=1, source_target_pairs={{16,0},{32,16},{48,32},{64,48},{80,64},{96,80},{112,96},{128,112},... | collective-permute-start | bytes 516104 | tf_op jit(solution)/shard_map/ppermute | solution.py:158
  20.0 7.8 %collective-permute-start.3 = (f32[2,168,128]{2,1,0:T(8,128)S(1)}, f32[2,168,128]{2,1,0:T(8,128)S(1)}, u32[]{:S(2)}, u32[]{:S(2)}) collective-permute-start(f32[2,168,128]{2,1,0:T(8,128)S(1)} %get-tuple-element.14), channel_id=1, source_target_pairs={{0,16},{16,32},{32,48},{48,64},{64,80},{80,96},{96,112},{112,128},... | collective-permute-start | bytes 516104 | tf_op jit(solution)/shard_map/ppermute | solution.py:158
  23.5 1.4 %copy-start.6 = (f32[3,2]{0,1:T(2,128)S(1)}, f32[3,2]{0,1:T(2,128)}, u32[]{:S(2)}) copy-start(f32[3,2]{0,1:T(2,128)} %param.9) | copy-start | bytes 76
  23.5 4.4 %collective-permute-start.5 = (f32[6,128]{1,0:T(8,128)S(1)}, f32[6,128]{1,0:T(8,128)S(1)}, u32[]{:S(2)}, u32[]{:S(2)}) collective-permute-start(f32[6,128]{1,0:T(8,128)S(1)} %pad_maximum_fusion.3), channel_id=1, source_target_pairs={{4,0},{8,4},{12,8},{5,1},{9,5},{13,9},{6,2},{10,6},{14,10},{7,3},{... | collective-permute-start | bytes 9224 | tf_op jit(solution)/shard_map/ppermute | solution.py:158
  25.2 2.7 %copy-start.2 = (f32[4,3]{1,0:T(4,128)S(1)}, f32[4,3]{1,0:T(4,128)}, u32[]{:S(2)}) copy-start(f32[4,3]{1,0:T(4,128)} %light_ref.1) | copy-start | bytes 148
  25.2 2.7 %copy-start.4 = (f32[4]{0:T(128)S(1)}, f32[4]{0:T(128)}, u32[]{:S(2)}) copy-start(f32[4]{0:T(128)} %rate_ref.1) | copy-start | bytes 52
  35.2 70.9 %copy-start.3 = (s32[4,32]{1,0:T(4,128)S(1)}, s32[4,32]{1,0:T(4,128)}, u32[]{:S(2)}) copy-start(s32[4,32]{1,0:T(4,128)} %order_ref.1) | copy-start | bytes 1540

commit v2 on v1

--- a/solution.py
+++ b/solution.py
@@ -19,12 +19,26 @@
 SMEM = pl.BlockSpec(memory_space=pltpu.SMEM)
 
 
+def pack_kernel(own_ref, last_ref, pack_ref):
+    lane = lax.broadcasted_iota(jnp.int32, (TILE, TILE), 1)
+    last_ref[...] = own_ref[:, TILE - HALO :]
+    for k in range(2):
+        pack_ref[k] = jnp.where(
+            lane < TILE // 2, pltpu.roll(own_ref[3 - k], TILE // 2, axis=1), own_ref[k]
+        )
+
+
+def left_margin(left_ref, k):
+    return left_ref[k] if k < 2 else pltpu.roll(left_ref[3 - k], TILE // 2, axis=1)
+
+
 def render_kernel(
-    moves_ref, light_ref, palette_ref, rate_ref,
+    shear_ref, offset_ref, light_ref, palette_ref, rate_ref,
     own_ref, above_ref, left_ref, corner_ref, front_ref, back_ref, below_ref, right_ref,
     out_ref,
     core_s, side_s, near_s, fields,
 ):
+    brick = lax.axis_index("gz")
     gy = lax.axis_index("gy")
     gx = lax.axis_index("gx")
     lane8 = lax.broadcasted_iota(jnp.int32, (8, TILE), 1)
@@ -33,25 +47,22 @@
         core_s[k, BASE : BASE + HALO] = above_ref[k]
         core_s[k, BASE + HALO : BASE + EXT] = own_ref[k]
         core_s[k, BASE + EXT : BASE + EXT + 1] = below_ref[k : k + 1]
-        pack = 0 if k in (0, 3) else 1
-        corner, left, below = corner_ref[pack], left_ref[pack], below_ref[4 + pack : 5 + pack]
+        side_s[k, BASE : BASE + HALO] = corner_ref[k]
+        side_s[k, BASE + HALO : BASE + EXT] = left_margin(left_ref, k)
+        row = jnp.broadcast_to(below_ref[BZ + min(k, 3 - k) : BZ + min(k, 3 - k) + 1], (8, TILE))
         if k >= 2:
-            corner = pltpu.roll(corner, 64, axis=1)
-            left = pltpu.roll(left, 64, axis=1)
-            below = pltpu.roll(jnp.broadcast_to(below, (8, TILE)), 64, axis=1)[0:1]
-        side_s[k, BASE : BASE + HALO] = corner
-        side_s[k, BASE + HALO : BASE + EXT] = left
-        side_s[k, BASE + EXT : BASE + EXT + 1] = below
-    near_s[0] = pltpu.roll(front_ref[1], 64, axis=1)
-    near_s[1] = back_ref[1]
+            row = pltpu.roll(row, TILE // 2, axis=1)
+        side_s[k, BASE + EXT : BASE + EXT + 1] = row[:1]
+    near_s[:HALO] = front_ref[1, :HALO]
+    near_s[HALO:] = pltpu.roll(front_ref[1, HALO:], TILE // 2, axis=1)
 
     def derive(i, carry):
         row = pl.multiple_of(i * 8, 8)
         at = pl.multiple_of(row + BASE, 8)
         core = [core_s[k, pl.ds(at, 8)] for k in range(BZ)]
         side = [side_s[k, pl.ds(at, 8)] for k in range(BZ)]
-        front = (front_ref[0, pl.ds(row, 8)], near_s[0, pl.ds(row, 8)])
-        back = (back_ref[0, pl.ds(row, 8)], near_s[1, pl.ds(row, 8)])
+        front = (front_ref[0, pl.ds(row, 8)], near_s[pl.ds(row, 8)])
+        back = (back_ref[0, pl.ds(row, 8)], back_ref[1, pl.ds(row, 8)])
         edge = right_ref[pl.ds(row, 8)]
         for k in range(BZ):
             c, s = core[k], side[k]
@@ -79,11 +90,11 @@
                 fields[2, k, half, pl.ds(row, 8)] = gr * factor
                 fields[3, k, half, pl.ds(row, 8)] = gc * factor
                 for c3 in range(3):
-                    arg = palette_ref[c3, 0] + palette_ref[c3, 1] * value
+                    arg = palette_ref[0, c3] + palette_ref[1, c3] * value
                     fields[4 + c3, k, half, pl.ds(row, 8)] = 0.5 + 0.5 * jnp.tanh(0.5 * arg)
         return carry
 
-    lax.fori_loop(0, EXT // 8, derive, 0)
+    lax.fori_loop(0, EXT // 8, derive, 0, unroll=3)
 
     lane = lax.broadcasted_iota(jnp.int32, (CHUNK, TILE), 1)
     rows = lax.broadcasted_iota(jnp.int32, (CHUNK, TILE), 0)
@@ -94,7 +105,7 @@
         length = jnp.sqrt(ld * ld + lr * lr + lc * lc + 1.0)
         td, tr, tc = ((v / length)[0:1] for v in (ld, lr, lc))
         rate = rate_ref[view]
-        off_r, off_c = moves_ref[view * 10 + 8], moves_ref[view * 10 + 9]
+        off_r, off_c = offset_ref[view, 0, brick], offset_ref[view, 1, brick]
 
         def shade_rows(j, carry, view=view, td=td, tr=tr, tc=tc, rate=rate, off_r=off_r, off_c=off_c):
             base = pl.multiple_of(j * CHUNK, CHUNK)
@@ -105,8 +116,8 @@
             clear = jnp.ones((CHUNK, TILE), jnp.float32)
             color = [jnp.zeros((CHUNK, TILE), jnp.float32) for _ in range(3)]
             for k in range(BZ):
-                dy = moves_ref[view * 10 + 2 * k]
-                dx = moves_ref[view * 10 + 2 * k + 1]
+                dy = off_r + shear_ref[view, 0, brick * BZ + k]
+                dx = off_c + shear_ref[view, 1, brick * BZ + k]
                 start = base + (HALO - dy)
                 own = lane < TILE - dx
 
@@ -131,7 +142,7 @@
                     )
             return carry
 
-        lax.fori_loop(0, TILE // CHUNK, shade_rows, 0)
+        lax.fori_loop(0, TILE // CHUNK, shade_rows, 0, unroll=True)
 
 
 def composite_kernel(order_ref, pieces_ref, out_ref):
@@ -168,35 +179,32 @@
 
 def on_device(pressure, light, palette, rate, shear, offset, order):
     bricks = order.shape[1]
-    brick = lax.axis_index("gz")
-    zero = jnp.zeros((), jnp.int32)
-
-    shifts = lax.dynamic_slice(shear, (zero, brick * BZ, zero), (VIEWS, BZ, 2))
-    place = lax.dynamic_slice(offset, (zero, brick, zero), (VIEWS, 1, 2))
-    moves = jnp.concatenate([shifts + place, place], axis=1).reshape(-1)
-
-    half = TILE // 2
-    pack = jnp.concatenate(
-        [
-            jnp.stack([pressure[3, :, half:], pressure[2, :, half:]]),
-            jnp.stack([pressure[0, :, half:], pressure[1, :, half:]]),
-        ],
-        axis=2,
-    )
-    above = moved(pressure[:, TILE - HALO :], "gy", 1)
+
+    def shapes(*dims):
+        return [jax.ShapeDtypeStruct(dim, jnp.float32) for dim in dims]
+
+    last, pack = pl.pallas_call(
+        pack_kernel,
+        out_shape=shapes((BZ, HALO, TILE), (2, TILE, TILE)),
+        in_specs=[VMEM],
+        out_specs=[VMEM] * 2,
+        compiler_params=pltpu.CompilerParams(vmem_limit_bytes=8 * 1024 * 1024),
+        name="pack",
+    )(pressure)
+    above = moved(last, "gy", 1)
     left = moved(pack, "gx", 1)
-    corner = diagonal(pack[:, TILE - HALO :])
-
-    def slice_with_margins(k):
+    corner = diagonal(last)
+
+    def slice_with_margins(k, margin):
         return jnp.stack(
             [
                 jnp.concatenate([above[k], pressure[k]], axis=0),
-                jnp.concatenate([corner[0], left[0]], axis=0),
+                jnp.concatenate([corner[k], margin], axis=0),
             ]
         )
 
-    front = moved(slice_with_margins(3), "gz", 1)
-    back = moved(slice_with_margins(0), "gz", -1)
+    front = moved(slice_with_margins(3, left[0]), "gz", 1)
+    back = moved(slice_with_margins(0, left[0]), "gz", -1)
     below = moved(jnp.concatenate([pressure[:, 0], left[:, 0]], axis=0), "gy", -1)
     edge = jnp.concatenate(
         [jnp.concatenate([above[k, :, :32], pressure[k, :, :32]], axis=0) for k in range(BZ)], axis=1
@@ -206,17 +214,20 @@
     pieces = pl.pallas_call(
         render_kernel,
         out_shape=jax.ShapeDtypeStruct((bricks, 4 * VIEWS * 4, TILE), jnp.float32),
-        in_specs=[SMEM] * 4 + [VMEM] * 8,
+        in_specs=[SMEM] * 5 + [VMEM] * 8,
         out_specs=VMEM,
         scratch_shapes=[
             pltpu.VMEM((BZ, BASE + EXT + 8, TILE), jnp.float32),
             pltpu.VMEM((BZ, BASE + EXT + 8, TILE), jnp.float32),
-            pltpu.VMEM((2, EXT, TILE), jnp.float32),
+            pltpu.VMEM((EXT, TILE), jnp.float32),
             pltpu.VMEM((7, BZ, 2, EXT, TILE), jnp.float32),
         ],
         compiler_params=pltpu.CompilerParams(vmem_limit_bytes=32 * 1024 * 1024),
         name="render",
-    )(moves, light, palette, rate, pressure, above, left, corner, front, back, below, right)
+    )(
+        shear.transpose(0, 2, 1), offset.transpose(0, 2, 1), light, palette.T, rate, pressure, above, left,
+        corner, front, back, below, right,
+    )
 
     strips = lax.all_to_all(pieces, "gz", 0, 0, tiled=True)
 

time: 108 us -> 106 us (0.981)
  Pallas kernels: 8.67 us -> 5.39 us
  blocking collectives: 70.9 us -> 72.9 us
  local copies, waits for them, and re-layouts: 3.47 us -> 1.86 us
    pallas_call x1, Pallas kernels: 7.29 us -> 3.92 us  [on_device(): pl.pallas_call(render_kernel, out_shape=jax.ShapeDtypeStruct((bricks, 4 *...]
    all_to_all x1, blocking collectives: 70.9 us -> 72.9 us  [on_device(): strips = lax.all_to_all(pieces, 'gz', 0, 0, tiled=True)]
  transfers between devices with their start and end apart: 7 -> 7, of which waited for: 1 -> 3; matrix products, arithmetic and copies ran while one was open for 2% -> 0% of each run, Pallas kernels for 0% -> 0%
where the time goes in v2:
time: 106 us
  blocking collectives  72.9 us (69%)
  starting transfers between devices  21.6 us (20%)
  Pallas kernels  5.39 us (5%)
  waiting for transfers between devices  3.52 us (3%)
  local copies, waits for them, and re-layouts  1.86 us (2%)
    all_to_all x1, blocking collectives, on_device(): strips = lax.all_to_all(pieces, 'gz', 0, 0, tiled=True)  72.9 us
    ppermute x6, starting transfers between devices, moved(): lax.ppermute(value, axes, [(i, i + steps) for i in range(first, last)])  17.5 us
    ppermute x1, starting transfers between devices, diagonal(): return lax.ppermute(value, ('gy', 'gx'), pairs)  4.13 us
    pallas_call x1, Pallas kernels, on_device(): pl.pallas_call(render_kernel, out_shape=jax.ShapeDtypeStruct((bricks, 4 *...  3.92 us
    ppermute x6, waiting for transfers between devices, moved(): lax.ppermute(value, axes, [(i, i + steps) for i in range(first, last)])  3.52 us
  transfers between devices with their start and end apart: 7, of which 3 were waited for; matrix products, arithmetic and copies ran while one was open for 0% of the time, Pallas kernels for 0%

profile of v2, /device:TPU:3, one launch (start us, length us, event | category | flops | bytes accessed | tf_op | source)
XLA Modules:
  0.0 105.8 jit_solution(5840776983575560519)
XLA Ops:
  0.0 0.9 copy-done
  1.0 0.1 pack.1
  1.1 4.1 %collective-permute-start.2 = (f32[4,40,128]{2,1,0:T(8,128)S(1)}, f32[4,40,128]{2,1,0:T(8,128)S(1)}, u32[]{:S(2)}, u32[]{:S(2)}) collective-permute-start(f32[4,40,128]{2,1,0:T(8,128)S(1)} %get-tuple-element.7), channel_id=1, source_target_pairs={{0,5},{1,6},{2,7},{4,9},{5,10},{6,11},{8,13},{9,14},{10,15},{16,21... | collective-permute-start | bytes 245768 | tf_op jit(solution)/shard_map/ppermute | solution.py:177
  5.2 3.2 %collective-permute-start = (f32[4,40,128]{2,1,0:T(8,128)S(1)}, f32[4,40,128]{2,1,0:T(8,128)S(1)}, u32[]{:S(2)}, u32[]{:S(2)}) collective-permute-start(f32[4,40,128]{2,1,0:T(8,128)S(1)} %get-tuple-element.7), channel_id=1, source_target_pairs={{0,4},{4,8},{8,12},{1,5},{5,9},{9,13},{2,6},{6,10},{10,14},{3,7},{... | collective-permute-start | bytes 245768 | tf_op jit(solution)/shard_map/ppermute | solution.py:169
  8.4 0.1 copy.26
  8.5 2.8 %collective-permute-start.1 = (f32[2,128,128]{2,0,1:T(2,128)S(1)}, f32[2,128,128]{2,0,1:T(2,128)S(1)}, u32[]{:S(2)}, u32[]{:S(2)}) collective-permute-start(f32[2,128,128]{2,0,1:T(2,128)S(1)} %copy.26), channel_id=1, source_target_pairs={{0,1},{1,2},{2,3},{4,5},{5,6},{6,7},{8,9},{9,10},{10,11},{12,13},{... | collective-permute-start | bytes 393224 | tf_op jit(solution)/shard_map/ppermute | solution.py:169
  11.4 0.0 collective-permute-done.above_ref
  11.4 0.1 maximum_maximum_fusion
  11.6 2.5 %collective-permute-start.6 = (f32[168,128]{1,0:T(8,128)S(1)}, f32[168,128]{1,0:T(8,128)S(1)}, u32[]{:S(2)}, u32[]{:S(2)}) collective-permute-start(f32[168,128]{1,0:T(8,128)S(1)} %maximum_maximum_fusion), channel_id=1, source_target_pairs={{1,0},{2,1},{3,2},{5,4},{6,5},{7,6},{9,8},{10,9},{11,10},{13,12},{... | collective-permute-start | bytes 258056 | tf_op jit(solution)/shard_map/ppermute | solution.py:169
  14.1 0.1 collective-permute-done.1
  14.3 5.8 %collective-permute-start.3 = (f32[2,168,128]{2,1,0:T(8,128)S(1)}, f32[2,168,128]{2,1,0:T(8,128)S(1)}, u32[]{:S(2)}, u32[]{:S(2)}) collective-permute-start(f32[2,168,128]{2,1,0:T(8,128)S(1)} %pad_maximum_fusion), channel_id=1, source_target_pairs={{0,16},{16,32},{32,48},{48,64},{64,80},{80,96},{96,112},{112,128},... | collective-permute-start | bytes 516104 | tf_op jit(solution)/shard_map/ppermute | solution.py:169
  20.2 1.9 %collective-permute-start.4 = (f32[2,168,128]{2,1,0:T(8,128)S(1)}, f32[2,168,128]{2,1,0:T(8,128)S(1)}, u32[]{:S(2)}, u32[]{:S(2)}) collective-permute-start(f32[2,168,128]{2,1,0:T(8,128)S(1)} %pad_maximum_fusion.1), channel_id=1, source_target_pairs={{16,0},{32,16},{48,32},{64,48},{80,64},{96,80},{112,96},{128,112},... | collective-permute-start | bytes 516104 | tf_op jit(solution)/shard_map/ppermute | solution.py:169
  22.1 1.3 %collective-permute-start.5 = (f32[6,128]{1,0:T(8,128)S(1)}, f32[6,128]{1,0:T(8,128)S(1)}, u32[]{:S(2)}, u32[]{:S(2)}) collective-permute-start(f32[6,128]{1,0:T(8,128)S(1)} %pad_maximum_fusion.4), channel_id=1, source_target_pairs={{4,0},{8,4},{12,8},{5,1},{9,5},{13,9},{6,2},{10,6},{14,10},{7,3},{... | collective-permute-start | bytes 9224 | tf_op jit(solution)/shard_map/ppermute | solution.py:169
  23.4 0.0 copy-start.3
  23.4 0.0 copy-start.4
  23.5 0.0 copy-start.2
  23.5 3.0 %collective-permute-done.5.below_ref = f32[6,128]{1,0:T(8,128)S(1)} collective-permute-done((f32[6,128]{1,0:T(8,128)S(1)}, f32[6,128]{1,0:T(8,128)S(1)}, u32[]{:S(2)}, u32[]{:S(2)}) %collective-permute-start.5) | collective-permute-done | bytes 3104 | tf_op jit(solution)/shard_map/ppermute | solution.py:169
  26.5 0.0 collective-permute-done.3.front_ref
  26.5 0.4 collective-permute-done.4.back_ref
  26.9 0.7 copy-done.6
  27.6 3.9 %render.1 = f32[32,64,128]{2,1,0:T(8,128)S(1)} custom-call(s32[4,2,128]{2,1,0:T(2,128)S(1)} %bitcast.45, s32[4,2,32]{2,1,0:T(2,128)S(1)} %bitcast.46, f32[4,3]{1,0:T(4,128)S(1)} %copy-done.4, f32[2,3]{1,0:T(2,128)S(1)} %bitcast.47, f32[4]{0:T(128)S(1)} %copy-done.7, f32[4,128,128]{2,1,0:T(8,128)S(1)} %copy-done.1, ...), custom_call_target="tpu_custom_call" | custom-call | tf_op jit(solution)/shard_map/render/pallas_call | solution.py:214
  31.5 0.0 copy-start.5
  31.5 72.9 %all_to_all.5.pieces_ref = f32[32,64,128]{2,1,0:T(8,128)S(1)} all-to-all(f32[32,64,128]{2,1,0:T(8,128)S(1)} %render.1), channel_id=1, replica_groups=mesh['gz'=32,'gy'=4,'gx'=4] {'gz'}, dimensions={0} | all-to-all | bytes 2097152 | tf_op jit(solution)/shard_map/all_to_all | solution.py:232
  104.4 1.4 %composite.1 = f32[4,4,1,4,128]{4,3,2,1,0:T(4,128)} custom-call(s32[4,32]{1,0:T(4,128)S(1)} %copy-done.5, f32[32,64,128]{2,1,0:T(8,128)S(1)} %all_to_all.5.pieces_ref), custom_call_target="tpu_custom_call" | custom-call | tf_op jit(solution)/shard_map/composite/pallas_call | solution.py:234
  (27 shorter events, 0.2 us)
Async XLA Ops:
  0.0 0.9 copy-start
  1.0 10.4 %copy-start.1 = (f32[4,128,128]{2,1,0:T(8,128)S(1)}, f32[4,128,128]{2,1,0:T(8,128)}, u32[]{:S(2)}) copy-start(f32[4,128,128]{2,1,0:T(8,128)} %own_ref.3) | copy-start | bytes 786436
  1.1 13.0 %collective-permute-start.2 = (f32[4,40,128]{2,1,0:T(8,128)S(1)}, f32[4,40,128]{2,1,0:T(8,128)S(1)}, u32[]{:S(2)}, u32[]{:S(2)}) collective-permute-start(f32[4,40,128]{2,1,0:T(8,128)S(1)} %get-tuple-element.7), channel_id=1, source_target_pairs={{0,5},{1,6},{2,7},{4,9},{5,10},{6,11},{8,13},{9,14},{10,15},{16,21... | collective-permute-start | bytes 245768 | tf_op jit(solution)/shard_map/ppermute | solution.py:177
  5.2 6.2 %collective-permute-start = (f32[4,40,128]{2,1,0:T(8,128)S(1)}, f32[4,40,128]{2,1,0:T(8,128)S(1)}, u32[]{:S(2)}, u32[]{:S(2)}) collective-permute-start(f32[4,40,128]{2,1,0:T(8,128)S(1)} %get-tuple-element.7), channel_id=1, source_target_pairs={{0,4},{4,8},{8,12},{1,5},{5,9},{9,13},{2,6},{6,10},{10,14},{3,7},{... | collective-permute-start | bytes 245768 | tf_op jit(solution)/shard_map/ppermute | solution.py:169
  8.5 5.7 %collective-permute-start.1 = (f32[2,128,128]{2,0,1:T(2,128)S(1)}, f32[2,128,128]{2,0,1:T(2,128)S(1)}, u32[]{:S(2)}, u32[]{:S(2)}) collective-permute-start(f32[2,128,128]{2,0,1:T(2,128)S(1)} %copy.26), channel_id=1, source_target_pairs={{0,1},{1,2},{2,3},{4,5},{5,6},{6,7},{8,9},{9,10},{10,11},{12,13},{... | collective-permute-start | bytes 393224 | tf_op jit(solution)/shard_map/ppermute | solution.py:169
  11.6 14.9 %collective-permute-start.6 = (f32[168,128]{1,0:T(8,128)S(1)}, f32[168,128]{1,0:T(8,128)S(1)}, u32[]{:S(2)}, u32[]{:S(2)}) collective-permute-start(f32[168,128]{1,0:T(8,128)S(1)} %maximum_maximum_fusion), channel_id=1, source_target_pairs={{1,0},{2,1},{3,2},{5,4},{6,5},{7,6},{9,8},{10,9},{11,10},{13,12},{... | collective-permute-start | bytes 258056 | tf_op jit(solution)/shard_map/ppermute | solution.py:169
  14.3 12.2 %collective-permute-start.3 = (f32[2,168,128]{2,1,0:T(8,128)S(1)}, f32[2,168,128]{2,1,0:T(8,128)S(1)}, u32[]{:S(2)}, u32[]{:S(2)}) collective-permute-start(f32[2,168,128]{2,1,0:T(8,128)S(1)} %pad_maximum_fusion), channel_id=1, source_target_pairs={{0,16},{16,32},{32,48},{48,64},{64,80},{80,96},{96,112},{112,128},... | collective-permute-start | bytes 516104 | tf_op jit(solution)/shard_map/ppermute | solution.py:169
  20.2 6.7 %collective-permute-start.4 = (f32[2,168,128]{2,1,0:T(8,128)S(1)}, f32[2,168,128]{2,1,0:T(8,128)S(1)}, u32[]{:S(2)}, u32[]{:S(2)}) collective-permute-start(f32[2,168,128]{2,1,0:T(8,128)S(1)} %pad_maximum_fusion.1), channel_id=1, source_target_pairs={{16,0},{32,16},{48,32},{64,48},{80,64},{96,80},{112,96},{128,112},... | collective-permute-start | bytes 516104 | tf_op jit(solution)/shard_map/ppermute | solution.py:169
  22.1 4.4 %collective-permute-start.5 = (f32[6,128]{1,0:T(8,128)S(1)}, f32[6,128]{1,0:T(8,128)S(1)}, u32[]{:S(2)}, u32[]{:S(2)}) collective-permute-start(f32[6,128]{1,0:T(8,128)S(1)} %pad_maximum_fusion.4), channel_id=1, source_target_pairs={{4,0},{8,4},{12,8},{5,1},{9,5},{13,9},{6,2},{10,6},{14,10},{7,3},{... | collective-permute-start | bytes 9224 | tf_op jit(solution)/shard_map/ppermute | solution.py:169
  23.4 3.5 %copy-start.3 = (s32[4,32,2]{1,2,0:T(2,128)S(1)}, s32[4,32,2]{1,2,0:T(2,128)}, u32[]{:S(2)}) copy-start(s32[4,32,2]{1,2,0:T(2,128)} %param.12) | copy-start | bytes 3076
  23.4 3.5 %copy-start.4 = (f32[4,3]{1,0:T(4,128)S(1)}, f32[4,3]{1,0:T(4,128)}, u32[]{:S(2)}) copy-start(f32[4,3]{1,0:T(4,128)} %light_ref.1) | copy-start | bytes 148
  23.5 3.4 %copy-start.2 = (s32[4,128,2]{1,2,0:T(2,128)S(1)}, s32[4,128,2]{1,2,0:T(2,128)}, u32[]{:S(2)}) copy-start(s32[4,128,2]{1,2,0:T(2,128)} %param.11) | copy-start | bytes 12292
  26.9 0.7 copy-start.6
  26.9 0.7 copy-start.7
  31.5 72.9 %copy-start.5 = (s32[4,32]{1,0:T(4,128)S(1)}, s32[4,32]{1,0:T(4,128)}, u32[]{:S(2)}) copy-start(s32[4,32]{1,0:T(4,128)} %order_ref.1) | copy-start | bytes 1540

commit v3 on v2

v3 whole, which is shorter than its diff:
```python
import jax
import jax.numpy as jnp
from jax import lax
from jax.experimental import pallas as pl
from jax.experimental.pallas import tpu as pltpu
from jax.sharding import PartitionSpec as P

VIEWS = 4
BZ = 4
TILE = 128
HALO = 40
EXT = HALO + TILE
CHUNK = 16

VMEM = pl.BlockSpec(memory_space=pltpu.VMEM)
SMEM = pl.BlockSpec(memory_space=pltpu.SMEM)
MEDIUM = pltpu.CompilerParams(vmem_limit_bytes=20 * 1024 * 1024)
SMALL = pltpu.CompilerParams(vmem_limit_bytes=8 * 1024 * 1024)


def pack_kernel(own_ref, last_ref, pack_ref, copy_ref):
    lane = lax.broadcasted_iota(jnp.int32, (TILE, TILE), 1)
    last_ref[...] = own_ref[:, TILE - HALO :]
    copy_ref[...] = own_ref[...]
    for k in range(2):
        pack_ref[k] = jnp.where(
            lane < TILE // 2, pltpu.roll(own_ref[3 - k], TILE // 2, axis=1), own_ref[k]
        )


def left_margin(left_ref, k):
    return left_ref[k] if k < 2 else pltpu.roll(left_ref[3 - k], TILE // 2, axis=1)


def inside_image(base, off_r, off_c):
    shape = (CHUNK, TILE)
    rows = lax.broadcasted_iota(jnp.int32, shape, 0) + (lax.axis_index("gy") * TILE + base)
    cols = lax.broadcasted_iota(jnp.int32, shape, 1) + lax.axis_index("gx") * TILE
    return jnp.logical_and(rows >= off_r, cols >= off_c)


def sampler(shear_ref, offset_ref, view, k, base):
    brick = lax.axis_index("gz")
    dy = offset_ref[view, 0, brick] + shear_ref[view, 0, brick * BZ + k]
    dx = offset_ref[view, 1, brick] + shear_ref[view, 1, brick * BZ + k]
    rows = pl.ds(base + (HALO - dy), CHUNK)
    own = lax.broadcasted_iota(jnp.int32, (CHUNK, TILE), 1) < TILE - dx

    def sample(ref, a):
        return pltpu.roll(jnp.where(own, ref[a, k, 0, rows], ref[a, k, 1, rows]), dx, axis=1)

    return sample


def store_strips(pieces_ref, base, row, value):
    for q in range(CHUNK // 4):
        pieces_ref[base // 4 + q, row : row + 4] = value[4 * q : 4 * q + 4]


def tone_kernel(
    shear_ref, offset_ref, palette_ref, rate_ref, own_ref, above_ref, left_ref, corner_ref,
    pieces_ref, tones_ref, cells_ref,
    fields,
):
    def tone(value, k, half, rows):
        cells_ref[k, half, rows] = value
        fields[0, k, half, rows] = jnp.tanh(value)
        for c3 in range(3):
            arg = palette_ref[0, c3] + palette_ref[1, c3] * value
            fields[1 + c3, k, half, rows] = 0.5 + 0.5 * jnp.tanh(0.5 * arg)

    for k in range(BZ):
        tone(above_ref[k], k, 0, slice(0, HALO))
        tone(own_ref[k], k, 0, slice(HALO, EXT))
        tone(corner_ref[k], k, 1, slice(0, HALO))
        tone(left_margin(left_ref, k), k, 1, slice(HALO, EXT))

    brick = lax.axis_index("gz")
    for view in range(VIEWS):
        off_r, off_c = offset_ref[view, 0, brick], offset_ref[view, 1, brick]
        rate = rate_ref[view]
        for base in range(0, TILE, CHUNK):
            depth = jnp.zeros((CHUNK, TILE), jnp.float32)
            clear = inside_image(base, off_r, off_c).astype(jnp.float32)
            inside = clear
            for k in range(BZ):
                sample = sampler(shear_ref, offset_ref, view, k, base)
                density = rate * (1.0 + sample(fields, 0))
                kept = clear * jnp.exp(-density)
                weight = clear - kept
                for c3 in range(3):
                    tones_ref[view, k, c3, base : base + CHUNK] = sample(fields, 1 + c3) * weight
                depth = depth + density
                clear = kept
            store_strips(pieces_ref, base, 48 + view * 4, depth * inside)


def render_kernel(
    shear_ref, offset_ref, light_ref,
    _, tones_ref, cells_ref, front_ref, back_ref, below_ref, right_ref,
    pieces_ref,
    normals,
):
    lane8 = lax.broadcasted_iota(jnp.int32, (8, TILE), 1)
    row8 = lax.broadcasted_iota(jnp.int32, (8, TILE), 0)

    for i in range(EXT // 8):
        row = slice(8 * i, 8 * i + 8)
        cells = [[cells_ref[k, half, row] for half in range(2)] for k in range(BZ)]
        front = [front_ref[0, row], front_ref[1, row]]
        if 8 * i >= HALO:
            front[1] = pltpu.roll(front[1], TILE // 2, axis=1)
        back = [back_ref[0, row], back_ref[1, row]]
        edge = right_ref[row]
        for k in range(BZ):
            c, s = cells[k]
            c_next = pltpu.roll(c, TILE - 1, axis=1)
            s_prev = pltpu.roll(s, 1, axis=1)
            c_right = jnp.where(
                lane8 == TILE - 1, pltpu.roll(edge, TILE - 1 - 32 * k, axis=1), c_next
            )
            c_left = jnp.where(lane8 == 0, s_prev, pltpu.roll(c, 1, axis=1))
            s_right = jnp.where(lane8 == TILE - 1, c_next, pltpu.roll(s, TILE - 1, axis=1))
            before = front if k == 0 else cells[k - 1]
            after = back if k == BZ - 1 else cells[k + 1]
            for half, (right, left) in enumerate(((c_right, c_left), (s_right, s_prev))):
                if i == 0:
                    upper = pltpu.roll(cells[k][half], 1, axis=0)
                else:
                    upper = cells_ref[k, half, 8 * i - 1 : 8 * i + 7]
                if i < EXT // 8 - 1:
                    lower = cells_ref[k, half, 8 * i + 1 : 8 * i + 9]
                else:
                    at = k if half == 0 else BZ + min(k, 3 - k)
                    last = jnp.broadcast_to(below_ref[at : at + 1], (8, TILE))
                    if half == 1 and k >= 2:
                        last = pltpu.roll(last, TILE // 2, axis=1)
                    lower = jnp.where(row8 == 7, last, pltpu.roll(cells[k][half], 7, axis=0))
                gd = 0.5 * (after[half] - before[half])
                gr = 0.5 * (lower - upper)
                gc = 0.5 * (right - left)
                factor = lax.rsqrt(gd * gd + gr * gr + gc * gc + 1.0)
                normals[0, k, half, row] = gd * factor
                normals[1, k, half, row] = gr * factor
                normals[2, k, half, row] = gc * factor

    for view in range(VIEWS):
        ld = jnp.full((8, TILE), light_ref[view, 0], jnp.float32)
        lr = jnp.full((8, TILE), light_ref[view, 1], jnp.float32)
        lc = jnp.full((8, TILE), light_ref[view, 2], jnp.float32)
        length = jnp.sqrt(ld * ld + lr * lr + lc * lc + 1.0)
        td, tr, tc = ((v / length)[0:1] for v in (ld, lr, lc))
        for base in range(0, TILE, CHUNK):
            color = [jnp.zeros((CHUNK, TILE), jnp.float32) for _ in range(3)]
            for k in range(BZ):
                sample = sampler(shear_ref, offset_ref, view, k, base)
                dot = sample(normals, 0) * td + sample(normals, 1) * tr + sample(normals, 2) * tc
                shade = 0.25 + 0.75 * dot * dot
                for c3 in range(3):
                    color[c3] = color[c3] + tones_ref[view, k, c3, base : base + CHUNK] * shade
            for c3 in range(3):
                store_strips(pieces_ref, base, c3 * 16 + view * 4, color[c3])


def composite_kernel(order_ref, pieces_ref, out_ref):
    bricks = pieces_ref.shape[0]
    for view in range(VIEWS):
        cover = jnp.zeros((4, TILE), jnp.float32)
        color = [jnp.zeros((4, TILE), jnp.float32) for _ in range(3)]
        for place in range(bricks):
            brick = order_ref[view, place]
            clear = jnp.exp(-cover)
            for c3 in range(3):
                at = c3 * 16 + view * 4
                color[c3] = color[c3] + pieces_ref[brick, at : at + 4] * clear
            at = 48 + view * 4
            cover = cover + pieces_ref[brick, at : at + 4]
        for c3 in range(3):
            out_ref[view, c3, 0] = color[c3]
        out_ref[view, 3, 0] = 1.0 - jnp.exp(-cover)


def moved(value, axes, steps):
    count = lax.axis_size(axes)
    first, last = max(0, -steps), min(count, count - steps)
    return lax.ppermute(value, axes, [(i, i + steps) for i in range(first, last)])


def diagonal(value):
    n_y, n_x = lax.axis_size("gy"), lax.axis_size("gx")
    pairs = [
        (y * n_x + x, (y + 1) * n_x + x + 1) for y in range(n_y - 1) for x in range(n_x - 1)
    ]
    return lax.ppermute(value, ("gy", "gx"), pairs)


def on_device(pressure, light, palette, rate, shear, offset, order):
    bricks = order.shape[1]

    def shapes(*dims):
        return [jax.ShapeDtypeStruct(dim, jnp.float32) for dim in dims]

    last, pack, own = pl.pallas_call(
        pack_kernel,
        out_shape=shapes((BZ, HALO, TILE), (2, TILE, TILE), (BZ, TILE, TILE)),
        in_specs=[VMEM],
        out_specs=[VMEM] * 3,
        compiler_params=SMALL,
        name="pack",
    )(pressure)
    above = moved(last, "gy", 1)
    left = moved(pack, "gx", 1)
    corner = diagonal(last)

    def slice_with_margins(k, margin):
        return jnp.stack(
            [
                jnp.concatenate([above[k], own[k]], axis=0),
                jnp.concatenate([corner[k], margin], axis=0),
            ]
        )

    front = moved(slice_with_margins(3, left[0]), "gz", 1)
    back = moved(slice_with_margins(0, left[0]), "gz", -1)
    below = moved(jnp.concatenate([own[:, 0], left[:, 0]], axis=0), "gy", -1)
    edge = jnp.concatenate(
        [jnp.concatenate([above[k, :, :32], own[k, :, :32]], axis=0) for k in range(BZ)], axis=1
    )
    right = moved(edge, "gx", -1)

    shears, offsets = shear.transpose(0, 2, 1), offset.transpose(0, 2, 1)
    strips_shape = (bricks, 4 * VIEWS * 4, TILE)
    pieces, tones, cells = pl.pallas_call(
        tone_kernel,
        out_shape=shapes(strips_shape, (VIEWS, BZ, 3, TILE, TILE), (BZ, 2, EXT, TILE)),
        in_specs=[SMEM] * 4 + [VMEM] * 4,
        out_specs=[VMEM] * 3,
        scratch_shapes=[pltpu.VMEM((4, BZ, 2, EXT, TILE), jnp.float32)],
        compiler_params=MEDIUM,
        cost_estimate=pl.CostEstimate(
            flops=10**7, bytes_accessed=4 * 10**6, transcendentals=3 * 10**6
        ),
        name="tone",
    )(shears, offsets, palette.T, rate, own, above, left, corner)
    (pieces,) = pl.pallas_call(
        render_kernel,
        out_shape=shapes(strips_shape),
        in_specs=[SMEM] * 3 + [VMEM] * 7,
        out_specs=[VMEM],
        input_output_aliases={3: 0},
        scratch_shapes=[pltpu.VMEM((3, BZ, 2, EXT, TILE), jnp.float32)],
        compiler_params=MEDIUM,
        name="render",
    )(shears, offsets, light, pieces, tones, cells, front, back, below, right)

    strips = lax.all_to_all(pieces, "gz", 0, 0, tiled=True)

    return pl.pallas_call(
        composite_kernel,
        out_shape=jax.ShapeDtypeStruct((VIEWS, 4, 1, 4, TILE), jnp.float32),
        in_specs=[SMEM, VMEM],
        out_specs=VMEM,
        compiler_params=pltpu.CompilerParams(vmem_limit_bytes=16 * 1024 * 1024),
        name="composite",
    )(order, strips)


def solution(mesh):
    return jax.shard_map(
        on_device,
        mesh=mesh,
        in_specs=(P("gz", "gy", "gx"), P(), P(), P(), P(), P(), P()),
        out_specs=P(None, None, "gz", "gy", "gx"),
        check_vma=False,
    )
```

time: 106 us -> 104 us (0.981)
  waiting for transfers between devices: 3.52 us -> 0.93 us
    ppermute x6, waiting for transfers between devices: 3.52 us -> 0.92 us  [moved(): lax.ppermute(value, axes, [(i, i + steps) for i in range(first, last)])]
    pallas_call x1 -> x2, Pallas kernels: 3.92 us -> 4.8 us  [the longest x1 2.49 us: on_device(): pl.pallas_call(tone_kernel, out_shape=shapes(strips_shape, (VIEWS, BZ, 3,...]
  transfers between devices with their start and end apart: 7 -> 7, of which waited for: 3 -> 2; matrix products, arithmetic and copies ran while one was open for 0% -> 1% of each run, Pallas kernels for 0% -> 2%
where the time goes in v3:
time: 104 us
  blocking collectives  72.9 us (70%)
  starting transfers between devices  21.6 us (21%)
  Pallas kernels  6.28 us (6%)
  local copies, waits for them, and re-layouts  1.36 us (1%)
    all_to_all x1, blocking collectives, on_device(): strips = lax.all_to_all(pieces, 'gz', 0, 0, tiled=True)  72.9 us
    ppermute x6, starting transfers between devices, moved(): lax.ppermute(value, axes, [(i, i + steps) for i in range(first, last)])  17.4 us
    ppermute x1, starting transfers between devices, diagonal(): return lax.ppermute(value, ('gy', 'gx'), pairs)  4.13 us
    pallas_call x1, Pallas kernels, on_device(): pl.pallas_call(tone_kernel, out_shape=shapes(strips_shape, (VIEWS, BZ, 3,...  2.49 us
    pallas_call x1, Pallas kernels, on_device(): pl.pallas_call(render_kernel, out_shape=shapes(strips_shape), in_specs=[S...  2.32 us
  transfers between devices with their start and end apart: 7, of which 2 were waited for; matrix products, arithmetic and copies ran while one was open for 1% of the time, Pallas kernels for 2%

profile of v3, /device:TPU:3, one launch (start us, length us, event | category | flops | bytes accessed | tf_op | source)
XLA Modules:
  0.0 103.6 jit_solution(6672100305323538997)
XLA Ops:
  0.0 0.9 copy-done
  1.0 0.1 pack.1
  1.1 4.1 %collective-permute-start.2 = (f32[4,40,128]{2,1,0:T(8,128)S(1)}, f32[4,40,128]{2,1,0:T(8,128)S(1)}, u32[]{:S(2)}, u32[]{:S(2)}) collective-permute-start(f32[4,40,128]{2,1,0:T(8,128)S(1)} %get-tuple-element.12), channel_id=1, source_target_pairs={{0,5},{1,6},{2,7},{4,9},{5,10},{6,11},{8,13},{9,14},{10,15},{16,21... | collective-permute-start | bytes 245768 | tf_op jit(solution)/shard_map/ppermute | solution.py:194
  5.2 3.2 %collective-permute-start = (f32[4,40,128]{2,1,0:T(8,128)S(1)}, f32[4,40,128]{2,1,0:T(8,128)S(1)}, u32[]{:S(2)}, u32[]{:S(2)}) collective-permute-start(f32[4,40,128]{2,1,0:T(8,128)S(1)} %get-tuple-element.12), channel_id=1, source_target_pairs={{0,4},{4,8},{8,12},{1,5},{5,9},{9,13},{2,6},{6,10},{10,14},{3,7},{... | collective-permute-start | bytes 245768 | tf_op jit(solution)/shard_map/ppermute | solution.py:186
  8.4 0.1 copy.27
  8.5 2.8 %collective-permute-start.1 = (f32[2,128,128]{2,0,1:T(2,128)S(1)}, f32[2,128,128]{2,0,1:T(2,128)S(1)}, u32[]{:S(2)}, u32[]{:S(2)}) collective-permute-start(f32[2,128,128]{2,0,1:T(2,128)S(1)} %copy.27), channel_id=1, source_target_pairs={{0,1},{1,2},{2,3},{4,5},{5,6},{6,7},{8,9},{9,10},{10,11},{12,13},{... | collective-permute-start | bytes 393224 | tf_op jit(solution)/shard_map/ppermute | solution.py:186
  11.4 0.2 copy.29
  11.6 0.0 collective-permute-done.above_ref
  11.6 0.1 maximum_maximum_fusion
  11.8 2.5 %collective-permute-start.6 = (f32[168,128]{1,0:T(8,128)S(1)}, f32[168,128]{1,0:T(8,128)S(1)}, u32[]{:S(2)}, u32[]{:S(2)}) collective-permute-start(f32[168,128]{1,0:T(8,128)S(1)} %maximum_maximum_fusion), channel_id=1, source_target_pairs={{1,0},{2,1},{3,2},{5,4},{6,5},{7,6},{9,8},{10,9},{11,10},{13,12},{... | collective-permute-start | bytes 258056 | tf_op jit(solution)/shard_map/ppermute | solution.py:186
  14.2 0.0 collective-permute-done.2.corner_ref
  14.3 0.0 collective-permute-done.1
  14.4 5.7 %collective-permute-start.3 = (f32[2,168,128]{2,1,0:T(8,128)S(1)}, f32[2,168,128]{2,1,0:T(8,128)S(1)}, u32[]{:S(2)}, u32[]{:S(2)}) collective-permute-start(f32[2,168,128]{2,1,0:T(8,128)S(1)} %pad_maximum_fusion), channel_id=1, source_target_pairs={{0,16},{16,32},{32,48},{48,64},{64,80},{80,96},{96,112},{112,128},... | collective-permute-start | bytes 516104 | tf_op jit(solution)/shard_map/ppermute | solution.py:186
  20.2 0.0 copy-start.3
  20.2 1.9 %collective-permute-start.4 = (f32[2,168,128]{2,1,0:T(8,128)S(1)}, f32[2,168,128]{2,1,0:T(8,128)S(1)}, u32[]{:S(2)}, u32[]{:S(2)}) collective-permute-start(f32[2,168,128]{2,1,0:T(8,128)S(1)} %pad_maximum_fusion.1), channel_id=1, source_target_pairs={{16,0},{32,16},{48,32},{64,48},{80,64},{96,80},{112,96},{128,112},... | collective-permute-start | bytes 516104 | tf_op jit(solution)/shard_map/ppermute | solution.py:186
  22.1 1.3 %collective-permute-start.5 = (f32[6,128]{1,0:T(8,128)S(1)}, f32[6,128]{1,0:T(8,128)S(1)}, u32[]{:S(2)}, u32[]{:S(2)}) collective-permute-start(f32[6,128]{1,0:T(8,128)S(1)} %pad_maximum_fusion.4), channel_id=1, source_target_pairs={{4,0},{8,4},{12,8},{5,1},{9,5},{13,9},{6,2},{10,6},{14,10},{7,3},{... | collective-permute-start | bytes 9224 | tf_op jit(solution)/shard_map/ppermute | solution.py:186
  23.5 2.5 %tone.1 = (f32[32,64,128]{2,1,0:T(8,128)S(1)}, f32[4,4,3,128,128]{4,3,2,1,0:T(8,128)S(1)}, f32[4,2,168,128]{3,2,1,0:T(8,128)S(1)}) custom-call(s32[4,2,128]{2,1,0:T(2,128)S(1)} %bitcast.44, s32[4,2,32]{2,1,0:T(2,128)S(1)} %bitcast.46, f32[2,3]{1,0:T(2,128)S(1)} %bitcast.48, f32[4]{0:T(128)S(1)} %copy-done.6, f32[4,128,128]{2,1,0:T(8,128)S(1)} %get-tuple-element.11.own_ref, ...), custom_call_target="tpu_custom_call" | custom-call | flops 10000000 | bytes 4000000 | tf_op jit(solution)/shard_map/tone/pallas_call | solution.py:233
  26.0 0.5 collective-permute-done.5.below_ref
  26.5 0.0 collective-permute-done.6.right_ref
  26.5 0.0 collective-permute-done.3.front_ref
  26.5 0.4 collective-permute-done.4.back_ref
  26.9 2.3 %render.1 = f32[32,64,128]{2,1,0:T(8,128)S(1)} custom-call(s32[4,2,128]{2,1,0:T(2,128)S(1)} %bitcast.45, s32[4,2,32]{2,1,0:T(2,128)S(1)} %bitcast.47, f32[4,3]{1,0:T(4,128)S(1)} %copy-done.3, f32[32,64,128]{2,1,0:T(8,128)S(1)} %get-tuple-element.14._, f32[4,4,3,128,128]{4,3,2,1,0:T(8,128)S(1)} %get-tuple-element.15.tones_ref, ...), custom_call_target="tpu_custom_call", output_to_operand_aliasing={{}: (3, {})} | custom-call | tf_op jit(solution)/shard_map/render/pallas_call | solution.py:245
  29.2 72.9 %all_to_all.5.pieces_ref = f32[32,64,128]{2,1,0:T(8,128)S(1)} all-to-all(f32[32,64,128]{2,1,0:T(8,128)S(1)} %render.1), channel_id=1, replica_groups=mesh['gz'=32,'gy'=4,'gx'=4] {'gz'}, dimensions={0} | all-to-all | bytes 2097152 | tf_op jit(solution)/shard_map/all_to_all | solution.py:256
  102.2 1.4 %composite.1 = f32[4,4,1,4,128]{4,3,2,1,0:T(4,128)} custom-call(s32[4,32]{1,0:T(4,128)S(1)} %copy-done.4, f32[32,64,128]{2,1,0:T(8,128)S(1)} %all_to_all.5.pieces_ref), custom_call_target="tpu_custom_call" | custom-call | tf_op jit(solution)/shard_map/composite/pallas_call | solution.py:258
  (27 shorter events, 0.2 us)
Async XLA Ops:
  0.0 0.9 copy-start
  1.0 22.5 %copy-start.1 = (s32[4,128,2]{1,2,0:T(2,128)S(1)}, s32[4,128,2]{1,2,0:T(2,128)}, u32[]{:S(2)}) copy-start(s32[4,128,2]{1,2,0:T(2,128)} %param.11) | copy-start | bytes 12292
  1.0 22.5 %copy-start.2 = (s32[4,32,2]{1,2,0:T(2,128)S(1)}, s32[4,32,2]{1,2,0:T(2,128)}, u32[]{:S(2)}) copy-start(s32[4,32,2]{1,2,0:T(2,128)} %param.12) | copy-start | bytes 3076
  1.0 22.5 %copy-start.5 = (f32[3,2]{0,1:T(2,128)S(1)}, f32[3,2]{0,1:T(2,128)}, u32[]{:S(2)}) copy-start(f32[3,2]{0,1:T(2,128)} %param.9) | copy-start | bytes 76
  1.0 22.5 %copy-start.6 = (f32[4]{0:T(128)S(1)}, f32[4]{0:T(128)}, u32[]{:S(2)}) copy-start(f32[4]{0:T(128)} %rate_ref.1) | copy-start | bytes 52
  1.1 13.2 %collective-permute-start.2 = (f32[4,40,128]{2,1,0:T(8,128)S(1)}, f32[4,40,128]{2,1,0:T(8,128)S(1)}, u32[]{:S(2)}, u32[]{:S(2)}) collective-permute-start(f32[4,40,128]{2,1,0:T(8,128)S(1)} %get-tuple-element.12), channel_id=1, source_target_pairs={{0,5},{1,6},{2,7},{4,9},{5,10},{6,11},{8,13},{9,14},{10,15},{16,21... | collective-permute-start | bytes 245768 | tf_op jit(solution)/shard_map/ppermute | solution.py:194
  5.2 6.4 %collective-permute-start = (f32[4,40,128]{2,1,0:T(8,128)S(1)}, f32[4,40,128]{2,1,0:T(8,128)S(1)}, u32[]{:S(2)}, u32[]{:S(2)}) collective-permute-start(f32[4,40,128]{2,1,0:T(8,128)S(1)} %get-tuple-element.12), channel_id=1, source_target_pairs={{0,4},{4,8},{8,12},{1,5},{5,9},{9,13},{2,6},{6,10},{10,14},{3,7},{... | collective-permute-start | bytes 245768 | tf_op jit(solution)/shard_map/ppermute | solution.py:186
  8.5 5.8 %collective-permute-start.1 = (f32[2,128,128]{2,0,1:T(2,128)S(1)}, f32[2,128,128]{2,0,1:T(2,128)S(1)}, u32[]{:S(2)}, u32[]{:S(2)}) collective-permute-start(f32[2,128,128]{2,0,1:T(2,128)S(1)} %copy.27), channel_id=1, source_target_pairs={{0,1},{1,2},{2,3},{4,5},{5,6},{6,7},{8,9},{9,10},{10,11},{12,13},{... | collective-permute-start | bytes 393224 | tf_op jit(solution)/shard_map/ppermute | solution.py:186
  11.8 14.7 %collective-permute-start.6 = (f32[168,128]{1,0:T(8,128)S(1)}, f32[168,128]{1,0:T(8,128)S(1)}, u32[]{:S(2)}, u32[]{:S(2)}) collective-permute-start(f32[168,128]{1,0:T(8,128)S(1)} %maximum_maximum_fusion), channel_id=1, source_target_pairs={{1,0},{2,1},{3,2},{5,4},{6,5},{7,6},{9,8},{10,9},{11,10},{13,12},{... | collective-permute-start | bytes 258056 | tf_op jit(solution)/shard_map/ppermute | solution.py:186
  14.4 12.1 %collective-permute-start.3 = (f32[2,168,128]{2,1,0:T(8,128)S(1)}, f32[2,168,128]{2,1,0:T(8,128)S(1)}, u32[]{:S(2)}, u32[]{:S(2)}) collective-permute-start(f32[2,168,128]{2,1,0:T(8,128)S(1)} %pad_maximum_fusion), channel_id=1, source_target_pairs={{0,16},{16,32},{32,48},{48,64},{64,80},{80,96},{96,112},{112,128},... | collective-permute-start | bytes 516104 | tf_op jit(solution)/shard_map/ppermute | solution.py:186
  20.2 6.8 %copy-start.3 = (f32[4,3]{1,0:T(4,128)S(1)}, f32[4,3]{1,0:T(4,128)}, u32[]{:S(2)}) copy-start(f32[4,3]{1,0:T(4,128)} %light_ref.1) | copy-start | bytes 148
  20.2 6.7 %collective-permute-start.4 = (f32[2,168,128]{2,1,0:T(8,128)S(1)}, f32[2,168,128]{2,1,0:T(8,128)S(1)}, u32[]{:S(2)}, u32[]{:S(2)}) collective-permute-start(f32[2,168,128]{2,1,0:T(8,128)S(1)} %pad_maximum_fusion.1), channel_id=1, source_target_pairs={{16,0},{32,16},{48,32},{64,48},{80,64},{96,80},{112,96},{128,112},... | collective-permute-start | bytes 516104 | tf_op jit(solution)/shard_map/ppermute | solution.py:186
  22.1 4.4 %collective-permute-start.5 = (f32[6,128]{1,0:T(8,128)S(1)}, f32[6,128]{1,0:T(8,128)S(1)}, u32[]{:S(2)}, u32[]{:S(2)}) collective-permute-start(f32[6,128]{1,0:T(8,128)S(1)} %pad_maximum_fusion.4), channel_id=1, source_target_pairs={{4,0},{8,4},{12,8},{5,1},{9,5},{13,9},{6,2},{10,6},{14,10},{7,3},{... | collective-permute-start | bytes 9224 | tf_op jit(solution)/shard_map/ppermute | solution.py:186
  26.9 75.3 %copy-start.4 = (s32[4,32]{1,0:T(4,128)S(1)}, s32[4,32]{1,0:T(4,128)}, u32[]{:S(2)}) copy-start(s32[4,32]{1,0:T(4,128)} %order_ref.1) | copy-start | bytes 1540

commit v4 on v3

--- a/solution.py
+++ b/solution.py
@@ -97,20 +97,23 @@
 
 def render_kernel(
     shear_ref, offset_ref, light_ref,
-    _, tones_ref, cells_ref, front_ref, back_ref, below_ref, right_ref,
+    _, tones_ref, cells_ref, inner_ref, outer_ref, below_ref, right_ref,
     pieces_ref,
     normals,
 ):
     lane8 = lax.broadcasted_iota(jnp.int32, (8, TILE), 1)
     row8 = lax.broadcasted_iota(jnp.int32, (8, TILE), 0)
+    even = jnp.full((8, TILE), lax.axis_index("gz"), jnp.int32) % 2 == 0
 
     for i in range(EXT // 8):
         row = slice(8 * i, 8 * i + 8)
         cells = [[cells_ref[k, half, row] for half in range(2)] for k in range(BZ)]
-        front = [front_ref[0, row], front_ref[1, row]]
+        inner = [inner_ref[half, row] for half in range(2)]
+        outer = [outer_ref[half, row] for half in range(2)]
+        front = [jnp.where(even, b, a) for b, a in zip(outer, inner, strict=True)]
+        back = [jnp.where(even, a, b) for b, a in zip(outer, inner, strict=True)]
         if 8 * i >= HALO:
             front[1] = pltpu.roll(front[1], TILE // 2, axis=1)
-        back = [back_ref[0, row], back_ref[1, row]]
         edge = right_ref[row]
         for k in range(BZ):
             c, s = cells[k]
@@ -186,6 +189,11 @@
     return lax.ppermute(value, axes, [(i, i + steps) for i in range(first, last)])
 
 
+def swapped(value, axis, first):
+    lows = range(first, lax.axis_size(axis) - 1, 2)
+    return lax.ppermute(value, axis, [p for i in lows for p in ((i, i + 1), (i + 1, i))])
+
+
 def diagonal(value):
     n_y, n_x = lax.axis_size("gy"), lax.axis_size("gx")
     pairs = [
@@ -220,8 +228,10 @@
             ]
         )
 
-    front = moved(slice_with_margins(3, left[0]), "gz", 1)
-    back = moved(slice_with_margins(0, left[0]), "gz", -1)
+    even = lax.axis_index("gz") % 2 == 0
+    first, final = slice_with_margins(0, left[0]), slice_with_margins(3, left[0])
+    inner = swapped(jnp.where(even, final, first), "gz", 0)
+    outer = swapped(jnp.where(even, first, final), "gz", 1)
     below = moved(jnp.concatenate([own[:, 0], left[:, 0]], axis=0), "gy", -1)
     edge = jnp.concatenate(
         [jnp.concatenate([above[k, :, :32], own[k, :, :32]], axis=0) for k in range(BZ)], axis=1
@@ -251,7 +261,7 @@
         scratch_shapes=[pltpu.VMEM((3, BZ, 2, EXT, TILE), jnp.float32)],
         compiler_params=MEDIUM,
         name="render",
-    )(shears, offsets, light, pieces, tones, cells, front, back, below, right)
+    )(shears, offsets, light, pieces, tones, cells, inner, outer, below, right)
 
     strips = lax.all_to_all(pieces, "gz", 0, 0, tiled=True)
 

time: 104 us -> 102 us (0.981)
  blocking collectives: 72.9 us -> 71.5 us
    ppermute x6 -> x4, starting transfers between devices: 17.4 us -> 9.78 us  [moved(): lax.ppermute(value, axes, [(i, i + steps) for i in range(first, last)])]
    ppermute x0 -> x2, starting transfers between devices: none -> 7.65 us  [swapped(): lax.ppermute(value, axis, [p for i in lows for p in ((i, i + 1), (i + 1,...]
    all_to_all x1, blocking collectives: 72.9 us -> 71.5 us  [on_device(): strips = lax.all_to_all(pieces, 'gz', 0, 0, tiled=True)]
  transfers between devices with their start and end apart: 7 -> 7, of which waited for: 2 -> 1; matrix products, arithmetic and copies ran while one was open for 1% -> 1% of each run, Pallas kernels for 2% -> 2%
where the time goes in v4:
time: 102 us
  blocking collectives  71.5 us (70%)
  starting transfers between devices  21.6 us (21%)
  Pallas kernels  6.3 us (6%)
  local copies, waits for them, and re-layouts  1.37 us (1%)
    all_to_all x1, blocking collectives, on_device(): strips = lax.all_to_all(pieces, 'gz', 0, 0, tiled=True)  71.5 us
    ppermute x4, starting transfers between devices, moved(): lax.ppermute(value, axes, [(i, i + steps) for i in range(first, last)])  9.78 us
    ppermute x2, starting transfers between devices, swapped(): lax.ppermute(value, axis, [p for i in lows for p in ((i, i + 1), (i + 1,...  7.65 us
    ppermute x1, starting transfers between devices, diagonal(): return lax.ppermute(value, ('gy', 'gx'), pairs)  4.13 us
    pallas_call x1, Pallas kernels, on_device(): pl.pallas_call(tone_kernel, out_shape=shapes(strips_shape, (VIEWS, BZ, 3,...  2.49 us
    pallas_call x1, Pallas kernels, on_device(): pl.pallas_call(render_kernel, out_shape=shapes(strips_shape), in_specs=[S...  2.33 us
  transfers between devices with their start and end apart: 7, of which 1 were waited for; matrix products, arithmetic and copies ran while one was open for 1% of the time, Pallas kernels for 2%

profile of v4, /device:TPU:3, one launch (start us, length us, event | category | flops | bytes accessed | tf_op | source)
XLA Modules:
  0.0 101.7 jit_solution(10346140389389840506)
XLA Ops:
  0.0 0.9 copy-done
  1.0 0.1 pack.1
  1.1 4.1 %collective-permute-start.2 = (f32[4,40,128]{2,1,0:T(8,128)S(1)}, f32[4,40,128]{2,1,0:T(8,128)S(1)}, u32[]{:S(2)}, u32[]{:S(2)}) collective-permute-start(f32[4,40,128]{2,1,0:T(8,128)S(1)} %get-tuple-element.12), channel_id=1, source_target_pairs={{0,5},{1,6},{2,7},{4,9},{5,10},{6,11},{8,13},{9,14},{10,15},{16,21... | collective-permute-start | bytes 245768 | tf_op jit(solution)/shard_map/ppermute | solution.py:202
  5.2 3.2 %collective-permute-start = (f32[4,40,128]{2,1,0:T(8,128)S(1)}, f32[4,40,128]{2,1,0:T(8,128)S(1)}, u32[]{:S(2)}, u32[]{:S(2)}) collective-permute-start(f32[4,40,128]{2,1,0:T(8,128)S(1)} %get-tuple-element.12), channel_id=1, source_target_pairs={{0,4},{4,8},{8,12},{1,5},{5,9},{9,13},{2,6},{6,10},{10,14},{3,7},{... | collective-permute-start | bytes 245768 | tf_op jit(solution)/shard_map/ppermute | solution.py:189
  8.4 0.1 copy.27
  8.5 2.8 %collective-permute-start.1 = (f32[2,128,128]{2,0,1:T(2,128)S(1)}, f32[2,128,128]{2,0,1:T(2,128)S(1)}, u32[]{:S(2)}, u32[]{:S(2)}) collective-permute-start(f32[2,128,128]{2,0,1:T(2,128)S(1)} %copy.27), channel_id=1, source_target_pairs={{0,1},{1,2},{2,3},{4,5},{5,6},{6,7},{8,9},{9,10},{10,11},{12,13},{... | collective-permute-start | bytes 393224 | tf_op jit(solution)/shard_map/ppermute | solution.py:189
  11.4 0.2 copy.29
  11.6 0.0 collective-permute-done.above_ref
  11.6 0.1 maximum_maximum_fusion
  11.8 2.5 %collective-permute-start.6 = (f32[168,128]{1,0:T(8,128)S(1)}, f32[168,128]{1,0:T(8,128)S(1)}, u32[]{:S(2)}, u32[]{:S(2)}) collective-permute-start(f32[168,128]{1,0:T(8,128)S(1)} %maximum_maximum_fusion), channel_id=1, source_target_pairs={{1,0},{2,1},{3,2},{5,4},{6,5},{7,6},{9,8},{10,9},{11,10},{13,12},{... | collective-permute-start | bytes 258056 | tf_op jit(solution)/shard_map/ppermute | solution.py:189
  14.3 0.0 collective-permute-done.2.corner_ref
  14.4 0.0 copy-start.3
  14.4 5.7 %collective-permute-start.4 = (f32[2,168,128]{2,1,0:T(8,128)S(1)}, f32[2,168,128]{2,1,0:T(8,128)S(1)}, u32[]{:S(2)}, u32[]{:S(2)}) collective-permute-start(f32[2,168,128]{2,1,0:T(8,128)S(1)} %get-tuple-element.17), channel_id=1, source_target_pairs={{16,32},{32,16},{48,64},{64,48},{80,96},{96,80},{112,128},{128,112... | collective-permute-start | bytes 516104 | tf_op jit(solution)/shard_map/ppermute | solution.py:194
  20.2 1.9 %collective-permute-start.3 = (f32[2,168,128]{2,1,0:T(8,128)S(1)}, f32[2,168,128]{2,1,0:T(8,128)S(1)}, u32[]{:S(2)}, u32[]{:S(2)}) collective-permute-start(f32[2,168,128]{2,1,0:T(8,128)S(1)} %get-tuple-element.18), channel_id=1, source_target_pairs={{0,16},{16,0},{32,48},{48,32},{64,80},{80,64},{96,112},{112,96},{1... | collective-permute-start | bytes 516104 | tf_op jit(solution)/shard_map/ppermute | solution.py:194
  22.1 1.3 %collective-permute-start.5 = (f32[6,128]{1,0:T(8,128)S(1)}, f32[6,128]{1,0:T(8,128)S(1)}, u32[]{:S(2)}, u32[]{:S(2)}) collective-permute-start(f32[6,128]{1,0:T(8,128)S(1)} %pad_maximum_fusion.4), channel_id=1, source_target_pairs={{4,0},{8,4},{12,8},{5,1},{9,5},{13,9},{6,2},{10,6},{14,10},{7,3},{... | collective-permute-start | bytes 9224 | tf_op jit(solution)/shard_map/ppermute | solution.py:189
  23.5 2.5 %tone.1 = (f32[32,64,128]{2,1,0:T(8,128)S(1)}, f32[4,4,3,128,128]{4,3,2,1,0:T(8,128)S(1)}, f32[4,2,168,128]{3,2,1,0:T(8,128)S(1)}) custom-call(s32[4,2,128]{2,1,0:T(2,128)S(1)} %bitcast.44, s32[4,2,32]{2,1,0:T(2,128)S(1)} %bitcast.46, f32[2,3]{1,0:T(2,128)S(1)} %bitcast.48, f32[4]{0:T(128)S(1)} %copy-done.6, f32[4,128,128]{2,1,0:T(8,128)S(1)} %get-tuple-element.11.own_ref, ...), custom_call_target="tpu_custom_call" | custom-call | flops 10000000 | bytes 4000000 | tf_op jit(solution)/shard_map/tone/pallas_call | solution.py:243
  26.0 0.5 collective-permute-done.5.below_ref
  26.5 0.0 collective-permute-done.6.right_ref
  26.5 0.0 collective-permute-done.4.outer_ref
  26.5 0.0 collective-permute-done.3.inner_ref
  26.5 0.0 copy-start.4
  26.5 2.3 %render.1 = f32[32,64,128]{2,1,0:T(8,128)S(1)} custom-call(s32[4,2,128]{2,1,0:T(2,128)S(1)} %bitcast.45, s32[4,2,32]{2,1,0:T(2,128)S(1)} %bitcast.47, f32[4,3]{1,0:T(4,128)S(1)} %copy-done.3, f32[32,64,128]{2,1,0:T(8,128)S(1)} %get-tuple-element.14._, f32[4,4,3,128,128]{4,3,2,1,0:T(8,128)S(1)} %get-tuple-element.15.tones_ref, ...), custom_call_target="tpu_custom_call", output_to_operand_aliasing={{}: (3, {})} | custom-call | tf_op jit(solution)/shard_map/render/pallas_call | solution.py:255
  28.9 71.5 %all_to_all.5.pieces_ref = f32[32,64,128]{2,1,0:T(8,128)S(1)} all-to-all(f32[32,64,128]{2,1,0:T(8,128)S(1)} %render.1), channel_id=1, replica_groups=mesh['gz'=32,'gy'=4,'gx'=4] {'gz'}, dimensions={0} | all-to-all | bytes 2097152 | tf_op jit(solution)/shard_map/all_to_all | solution.py:266
  100.4 1.4 %composite.1 = f32[4,4,1,4,128]{4,3,2,1,0:T(4,128)} custom-call(s32[4,32]{1,0:T(4,128)S(1)} %copy-done.4, f32[32,64,128]{2,1,0:T(8,128)S(1)} %all_to_all.5.pieces_ref), custom_call_target="tpu_custom_call" | custom-call | tf_op jit(solution)/shard_map/composite/pallas_call | solution.py:268
  (25 shorter events, 0.2 us)
Async XLA Ops:
  0.0 0.9 copy-start
  1.0 22.5 %copy-start.1 = (s32[4,128,2]{1,2,0:T(2,128)S(1)}, s32[4,128,2]{1,2,0:T(2,128)}, u32[]{:S(2)}) copy-start(s32[4,128,2]{1,2,0:T(2,128)} %param.11) | copy-start | bytes 12292
  1.0 22.5 %copy-start.2 = (s32[4,32,2]{1,2,0:T(2,128)S(1)}, s32[4,32,2]{1,2,0:T(2,128)}, u32[]{:S(2)}) copy-start(s32[4,32,2]{1,2,0:T(2,128)} %param.12) | copy-start | bytes 3076
  1.0 22.5 %copy-start.5 = (f32[3,2]{0,1:T(2,128)S(1)}, f32[3,2]{0,1:T(2,128)}, u32[]{:S(2)}) copy-start(f32[3,2]{0,1:T(2,128)} %param.9) | copy-start | bytes 76
  1.0 22.5 %copy-start.6 = (f32[4]{0:T(128)S(1)}, f32[4]{0:T(128)}, u32[]{:S(2)}) copy-start(f32[4]{0:T(128)} %rate_ref.1) | copy-start | bytes 52
  1.1 13.2 %collective-permute-start.2 = (f32[4,40,128]{2,1,0:T(8,128)S(1)}, f32[4,40,128]{2,1,0:T(8,128)S(1)}, u32[]{:S(2)}, u32[]{:S(2)}) collective-permute-start(f32[4,40,128]{2,1,0:T(8,128)S(1)} %get-tuple-element.12), channel_id=1, source_target_pairs={{0,5},{1,6},{2,7},{4,9},{5,10},{6,11},{8,13},{9,14},{10,15},{16,21... | collective-permute-start | bytes 245768 | tf_op jit(solution)/shard_map/ppermute | solution.py:202
  5.2 6.4 %collective-permute-start = (f32[4,40,128]{2,1,0:T(8,128)S(1)}, f32[4,40,128]{2,1,0:T(8,128)S(1)}, u32[]{:S(2)}, u32[]{:S(2)}) collective-permute-start(f32[4,40,128]{2,1,0:T(8,128)S(1)} %get-tuple-element.12), channel_id=1, source_target_pairs={{0,4},{4,8},{8,12},{1,5},{5,9},{9,13},{2,6},{6,10},{10,14},{3,7},{... | collective-permute-start | bytes 245768 | tf_op jit(solution)/shard_map/ppermute | solution.py:189
  8.5 5.8 %collective-permute-start.1 = (f32[2,128,128]{2,0,1:T(2,128)S(1)}, f32[2,128,128]{2,0,1:T(2,128)S(1)}, u32[]{:S(2)}, u32[]{:S(2)}) collective-permute-start(f32[2,128,128]{2,0,1:T(2,128)S(1)} %copy.27), channel_id=1, source_target_pairs={{0,1},{1,2},{2,3},{4,5},{5,6},{6,7},{8,9},{9,10},{10,11},{12,13},{... | collective-permute-start | bytes 393224 | tf_op jit(solution)/shard_map/ppermute | solution.py:189
  11.8 14.7 %collective-permute-start.6 = (f32[168,128]{1,0:T(8,128)S(1)}, f32[168,128]{1,0:T(8,128)S(1)}, u32[]{:S(2)}, u32[]{:S(2)}) collective-permute-start(f32[168,128]{1,0:T(8,128)S(1)} %maximum_maximum_fusion), channel_id=1, source_target_pairs={{1,0},{2,1},{3,2},{5,4},{6,5},{7,6},{9,8},{10,9},{11,10},{13,12},{... | collective-permute-start | bytes 258056 | tf_op jit(solution)/shard_map/ppermute | solution.py:189
  14.4 12.1 %copy-start.3 = (f32[4,3]{1,0:T(4,128)S(1)}, f32[4,3]{1,0:T(4,128)}, u32[]{:S(2)}) copy-start(f32[4,3]{1,0:T(4,128)} %light_ref.1) | copy-start | bytes 148
  14.4 12.1 %collective-permute-start.4 = (f32[2,168,128]{2,1,0:T(8,128)S(1)}, f32[2,168,128]{2,1,0:T(8,128)S(1)}, u32[]{:S(2)}, u32[]{:S(2)}) collective-permute-start(f32[2,168,128]{2,1,0:T(8,128)S(1)} %get-tuple-element.17), channel_id=1, source_target_pairs={{16,32},{32,16},{48,64},{64,48},{80,96},{96,80},{112,128},{128,112... | collective-permute-start | bytes 516104 | tf_op jit(solution)/shard_map/ppermute | solution.py:194
  20.2 6.3 %collective-permute-start.3 = (f32[2,168,128]{2,1,0:T(8,128)S(1)}, f32[2,168,128]{2,1,0:T(8,128)S(1)}, u32[]{:S(2)}, u32[]{:S(2)}) collective-permute-start(f32[2,168,128]{2,1,0:T(8,128)S(1)} %get-tuple-element.18), channel_id=1, source_target_pairs={{0,16},{16,0},{32,48},{48,32},{64,80},{80,64},{96,112},{112,96},{1... | collective-permute-start | bytes 516104 | tf_op jit(solution)/shard_map/ppermute | solution.py:194
  22.1 4.4 %collective-permute-start.5 = (f32[6,128]{1,0:T(8,128)S(1)}, f32[6,128]{1,0:T(8,128)S(1)}, u32[]{:S(2)}, u32[]{:S(2)}) collective-permute-start(f32[6,128]{1,0:T(8,128)S(1)} %pad_maximum_fusion.4), channel_id=1, source_target_pairs={{4,0},{8,4},{12,8},{5,1},{9,5},{13,9},{6,2},{10,6},{14,10},{7,3},{... | collective-permute-start | bytes 9224 | tf_op jit(solution)/shard_map/ppermute | solution.py:189
  26.5 73.9 %copy-start.4 = (s32[4,32]{1,0:T(4,128)S(1)}, s32[4,32]{1,0:T(4,128)}, u32[]{:S(2)}) copy-start(s32[4,32]{1,0:T(4,128)} %order_ref.1) | copy-start | bytes 1540

commit v5 on v4

--- a/solution.py
+++ b/solution.py
@@ -13,7 +13,6 @@
 CHUNK = 16
 
 VMEM = pl.BlockSpec(memory_space=pltpu.VMEM)
-SMEM = pl.BlockSpec(memory_space=pltpu.SMEM)
 MEDIUM = pltpu.CompilerParams(vmem_limit_bytes=20 * 1024 * 1024)
 SMALL = pltpu.CompilerParams(vmem_limit_bytes=8 * 1024 * 1024)
 
@@ -39,10 +38,19 @@
     return jnp.logical_and(rows >= off_r, cols >= off_c)
 
 
-def sampler(shear_ref, offset_ref, view, k, base):
+def moves_of(shear_ref, offset_ref):
     brick = lax.axis_index("gz")
-    dy = offset_ref[view, 0, brick] + shear_ref[view, 0, brick * BZ + k]
-    dx = offset_ref[view, 1, brick] + shear_ref[view, 1, brick * BZ + k]
+    shear = pltpu.roll(shear_ref[...], shear_ref.shape[2] - brick * BZ, axis=2)
+    offset = offset_ref[...]
+    here = lax.broadcasted_iota(jnp.int32, offset.shape, 2) == brick
+    place = jnp.sum(jnp.where(here, offset, 0), axis=2, keepdims=True)
+    total = shear + place
+    cells = [[(total[v, 0, k], total[v, 1, k]) for k in range(BZ)] for v in range(VIEWS)]
+    return cells, [(place[v, 0, 0], place[v, 1, 0]) for v in range(VIEWS)]
+
+
+def sampler(move, k, base):
+    dy, dx = move
     rows = pl.ds(base + (HALO - dy), CHUNK)
     own = lax.broadcasted_iota(jnp.int32, (CHUNK, TILE), 1) < TILE - dx
 
@@ -75,16 +83,16 @@
         tone(corner_ref[k], k, 1, slice(0, HALO))
         tone(left_margin(left_ref, k), k, 1, slice(HALO, EXT))
 
-    brick = lax.axis_index("gz")
+    moves, places = moves_of(shear_ref, offset_ref)
     for view in range(VIEWS):
-        off_r, off_c = offset_ref[view, 0, brick], offset_ref[view, 1, brick]
-        rate = rate_ref[view]
+        off_r, off_c = places[view]
+        rate = rate_ref[0, view]
         for base in range(0, TILE, CHUNK):
             depth = jnp.zeros((CHUNK, TILE), jnp.float32)
             clear = inside_image(base, off_r, off_c).astype(jnp.float32)
             inside = clear
             for k in range(BZ):
-                sample = sampler(shear_ref, offset_ref, view, k, base)
+                sample = sampler(moves[view][k], k, base)
                 density = rate * (1.0 + sample(fields, 0))
                 kept = clear * jnp.exp(-density)
                 weight = clear - kept
@@ -97,7 +105,7 @@
 
 def render_kernel(
     shear_ref, offset_ref, light_ref,
-    _, tones_ref, cells_ref, inner_ref, outer_ref, below_ref, right_ref,
+    started_ref, tones_ref, cells_ref, inner_ref, outer_ref, below_ref, right_ref,
     pieces_ref,
     normals,
 ):
@@ -147,6 +155,7 @@
                 normals[1, k, half, row] = gr * factor
                 normals[2, k, half, row] = gc * factor
 
+    moves, _ = moves_of(shear_ref, offset_ref)
     for view in range(VIEWS):
         ld = jnp.full((8, TILE), light_ref[view, 0], jnp.float32)
         lr = jnp.full((8, TILE), light_ref[view, 1], jnp.float32)
@@ -156,7 +165,7 @@
         for base in range(0, TILE, CHUNK):
             color = [jnp.zeros((CHUNK, TILE), jnp.float32) for _ in range(3)]
             for k in range(BZ):
-                sample = sampler(shear_ref, offset_ref, view, k, base)
+                sample = sampler(moves[view][k], k, base)
                 dot = sample(normals, 0) * td + sample(normals, 1) * tr + sample(normals, 2) * tc
                 shade = 0.25 + 0.75 * dot * dot
                 for c3 in range(3):
@@ -243,7 +252,7 @@
     pieces, tones, cells = pl.pallas_call(
         tone_kernel,
         out_shape=shapes(strips_shape, (VIEWS, BZ, 3, TILE, TILE), (BZ, 2, EXT, TILE)),
-        in_specs=[SMEM] * 4 + [VMEM] * 4,
+        in_specs=[VMEM] * 8,
         out_specs=[VMEM] * 3,
         scratch_shapes=[pltpu.VMEM((4, BZ, 2, EXT, TILE), jnp.float32)],
         compiler_params=MEDIUM,
@@ -251,11 +260,11 @@
             flops=10**7, bytes_accessed=4 * 10**6, transcendentals=3 * 10**6
         ),
         name="tone",
-    )(shears, offsets, palette.T, rate, own, above, left, corner)
+    )(shears, offsets, palette.T, rate[None], own, above, left, corner)
     (pieces,) = pl.pallas_call(
         render_kernel,
         out_shape=shapes(strips_shape),
-        in_specs=[SMEM] * 3 + [VMEM] * 7,
+        in_specs=[VMEM] * 10,
         out_specs=[VMEM],
         input_output_aliases={3: 0},
         scratch_shapes=[pltpu.VMEM((3, BZ, 2, EXT, TILE), jnp.float32)],
@@ -268,7 +277,7 @@
     return pl.pallas_call(
         composite_kernel,
         out_shape=jax.ShapeDtypeStruct((VIEWS, 4, 1, 4, TILE), jnp.float32),
-        in_specs=[SMEM, VMEM],
+        in_specs=[VMEM] * 2,
         out_specs=VMEM,
         compiler_params=pltpu.CompilerParams(vmem_limit_bytes=16 * 1024 * 1024),
         name="composite",

time: 102 us -> 101 us (level)
  Pallas kernels: 6.3 us -> 4.5 us
where the time goes in v5:
time: 101 us
  blocking collectives  71.5 us (71%)
  starting transfers between devices  21.6 us (21%)
  Pallas kernels  4.5 us (4%)
  local copies, waits for them, and re-layouts  1.37 us (1%)
  waiting for transfers between devices  1.2 us (1%)
    all_to_all x1, blocking collectives, on_device(): strips = lax.all_to_all(pieces, 'gz', 0, 0, tiled=True)  71.5 us
    ppermute x4, starting transfers between devices, moved(): lax.ppermute(value, axes, [(i, i + steps) for i in range(first, last)])  9.78 us
    ppermute x2, starting transfers between devices, swapped(): lax.ppermute(value, axis, [p for i in lows for p in ((i, i + 1), (i + 1,...  7.65 us
    ppermute x1, starting transfers between devices, diagonal(): return lax.ppermute(value, ('gy', 'gx'), pairs)  4.13 us
  transfers between devices with their start and end apart: 7, of which 1 were waited for; matrix products, arithmetic and copies ran while one was open for 1% of the time, Pallas kernels for 2%

profile of v5, /device:TPU:3, one launch (start us, length us, event | category | flops | bytes accessed | tf_op | source)
XLA Modules:
  0.0 100.7 jit_solution(7422554150331671706)
XLA Ops:
  0.0 0.9 copy-done
  1.0 0.1 pack.1
  1.1 4.1 %collective-permute-start.2 = (f32[4,40,128]{2,1,0:T(8,128)S(1)}, f32[4,40,128]{2,1,0:T(8,128)S(1)}, u32[]{:S(2)}, u32[]{:S(2)}) collective-permute-start(f32[4,40,128]{2,1,0:T(8,128)S(1)} %get-tuple-element.12), channel_id=1, source_target_pairs={{0,5},{1,6},{2,7},{4,9},{5,10},{6,11},{8,13},{9,14},{10,15},{16,21... | collective-permute-start | bytes 245768 | tf_op jit(solution)/shard_map/ppermute | solution.py:211
  5.2 3.2 %collective-permute-start = (f32[4,40,128]{2,1,0:T(8,128)S(1)}, f32[4,40,128]{2,1,0:T(8,128)S(1)}, u32[]{:S(2)}, u32[]{:S(2)}) collective-permute-start(f32[4,40,128]{2,1,0:T(8,128)S(1)} %get-tuple-element.12), channel_id=1, source_target_pairs={{0,4},{4,8},{8,12},{1,5},{5,9},{9,13},{2,6},{6,10},{10,14},{3,7},{... | collective-permute-start | bytes 245768 | tf_op jit(solution)/shard_map/ppermute | solution.py:198
  8.4 0.1 copy.27
  8.5 2.8 %collective-permute-start.1 = (f32[2,128,128]{2,0,1:T(2,128)S(1)}, f32[2,128,128]{2,0,1:T(2,128)S(1)}, u32[]{:S(2)}, u32[]{:S(2)}) collective-permute-start(f32[2,128,128]{2,0,1:T(2,128)S(1)} %copy.27), channel_id=1, source_target_pairs={{0,1},{1,2},{2,3},{4,5},{5,6},{6,7},{8,9},{9,10},{10,11},{12,13},{... | collective-permute-start | bytes 393224 | tf_op jit(solution)/shard_map/ppermute | solution.py:198
  11.4 0.2 copy.29
  11.6 0.0 collective-permute-done.above_ref
  11.6 0.1 maximum_maximum_fusion
  11.8 2.5 %collective-permute-start.6 = (f32[168,128]{1,0:T(8,128)S(1)}, f32[168,128]{1,0:T(8,128)S(1)}, u32[]{:S(2)}, u32[]{:S(2)}) collective-permute-start(f32[168,128]{1,0:T(8,128)S(1)} %maximum_maximum_fusion), channel_id=1, source_target_pairs={{1,0},{2,1},{3,2},{5,4},{6,5},{7,6},{9,8},{10,9},{11,10},{13,12},{... | collective-permute-start | bytes 258056 | tf_op jit(solution)/shard_map/ppermute | solution.py:198
  14.3 0.0 collective-permute-done.2.corner_ref
  14.4 0.0 copy-start.3
  14.4 5.7 %collective-permute-start.4 = (f32[2,168,128]{2,1,0:T(8,128)S(1)}, f32[2,168,128]{2,1,0:T(8,128)S(1)}, u32[]{:S(2)}, u32[]{:S(2)}) collective-permute-start(f32[2,168,128]{2,1,0:T(8,128)S(1)} %get-tuple-element.17), channel_id=1, source_target_pairs={{16,32},{32,16},{48,64},{64,48},{80,96},{96,80},{112,128},{128,112... | collective-permute-start | bytes 516104 | tf_op jit(solution)/shard_map/ppermute | solution.py:203
  20.2 1.9 %collective-permute-start.3 = (f32[2,168,128]{2,1,0:T(8,128)S(1)}, f32[2,168,128]{2,1,0:T(8,128)S(1)}, u32[]{:S(2)}, u32[]{:S(2)}) collective-permute-start(f32[2,168,128]{2,1,0:T(8,128)S(1)} %get-tuple-element.18), channel_id=1, source_target_pairs={{0,16},{16,0},{32,48},{48,32},{64,80},{80,64},{96,112},{112,96},{1... | collective-permute-start | bytes 516104 | tf_op jit(solution)/shard_map/ppermute | solution.py:203
  22.1 1.3 %collective-permute-start.5 = (f32[6,128]{1,0:T(8,128)S(1)}, f32[6,128]{1,0:T(8,128)S(1)}, u32[]{:S(2)}, u32[]{:S(2)}) collective-permute-start(f32[6,128]{1,0:T(8,128)S(1)} %pad_maximum_fusion.4), channel_id=1, source_target_pairs={{4,0},{8,4},{12,8},{5,1},{9,5},{13,9},{6,2},{10,6},{14,10},{7,3},{... | collective-permute-start | bytes 9224 | tf_op jit(solution)/shard_map/ppermute | solution.py:198
  23.5 1.8 %tone.1 = (f32[32,64,128]{2,1,0:T(8,128)S(1)}, f32[4,4,3,128,128]{4,3,2,1,0:T(8,128)S(1)}, f32[4,2,168,128]{3,2,1,0:T(8,128)S(1)}) custom-call(s32[4,2,128]{2,1,0:T(2,128)S(1)} %bitcast.45, s32[4,2,32]{2,1,0:T(2,128)S(1)} %bitcast.47, f32[2,3]{1,0:T(2,128)S(1)} %bitcast.49, f32[1,4]{1,0:T(1,128)S(1)} %bitcast.50, ...), custom_call_target="tpu_custom_call" | custom-call | flops 10000000 | bytes 4000000 | tf_op jit(solution)/shard_map/tone/pallas_call | solution.py:252
  25.3 1.2 %collective-permute-done.5.below_ref = f32[6,128]{1,0:T(8,128)S(1)} collective-permute-done((f32[6,128]{1,0:T(8,128)S(1)}, f32[6,128]{1,0:T(8,128)S(1)}, u32[]{:S(2)}, u32[]{:S(2)}) %collective-permute-start.5) | collective-permute-done | bytes 3104 | tf_op jit(solution)/shard_map/ppermute | solution.py:198
  26.5 0.0 collective-permute-done.6.right_ref
  26.5 0.0 collective-permute-done.4.outer_ref
  26.5 0.0 collective-permute-done.3.inner_ref
  26.5 0.0 copy-start.4
  26.5 1.7 %render.1 = f32[32,64,128]{2,1,0:T(8,128)S(1)} custom-call(s32[4,2,128]{2,1,0:T(2,128)S(1)} %bitcast.46, s32[4,2,32]{2,1,0:T(2,128)S(1)} %bitcast.48, f32[4,3]{1,0:T(4,128)S(1)} %copy-done.3, f32[32,64,128]{2,1,0:T(8,128)S(1)} %get-tuple-element.14.started_ref, ...), custom_call_target="tpu_custom_call", output_to_operand_aliasing={{}: (3, {})} | custom-call | tf_op jit(solution)/shard_map/render/pallas_call | solution.py:264
  28.2 71.5 %all_to_all.5.pieces_ref = f32[32,64,128]{2,1,0:T(8,128)S(1)} all-to-all(f32[32,64,128]{2,1,0:T(8,128)S(1)} %render.1), channel_id=1, replica_groups=mesh['gz'=32,'gy'=4,'gx'=4] {'gz'}, dimensions={0} | all-to-all | bytes 2097152 | tf_op jit(solution)/shard_map/all_to_all | solution.py:275
  99.7 0.9 composite.1
  (25 shorter events, 0.2 us)
Async XLA Ops:
  0.0 0.9 copy-start
  1.0 22.5 %copy-start.1 = (s32[4,128,2]{1,2,0:T(2,128)S(1)}, s32[4,128,2]{1,2,0:T(2,128)}, u32[]{:S(2)}) copy-start(s32[4,128,2]{1,2,0:T(2,128)} %param.11) | copy-start | bytes 12292
  1.0 22.5 %copy-start.2 = (s32[4,32,2]{1,2,0:T(2,128)S(1)}, s32[4,32,2]{1,2,0:T(2,128)}, u32[]{:S(2)}) copy-start(s32[4,32,2]{1,2,0:T(2,128)} %param.12) | copy-start | bytes 3076
  1.0 22.5 %copy-start.5 = (f32[3,2]{0,1:T(2,128)S(1)}, f32[3,2]{0,1:T(2,128)}, u32[]{:S(2)}) copy-start(f32[3,2]{0,1:T(2,128)} %param.9) | copy-start | bytes 76
  1.0 22.5 %copy-start.6 = (f32[4]{0:T(128)S(1)}, f32[4]{0:T(128)}, u32[]{:S(2)}) copy-start(f32[4]{0:T(128)} %param.10) | copy-start | bytes 52
  1.1 13.2 %collective-permute-start.2 = (f32[4,40,128]{2,1,0:T(8,128)S(1)}, f32[4,40,128]{2,1,0:T(8,128)S(1)}, u32[]{:S(2)}, u32[]{:S(2)}) collective-permute-start(f32[4,40,128]{2,1,0:T(8,128)S(1)} %get-tuple-element.12), channel_id=1, source_target_pairs={{0,5},{1,6},{2,7},{4,9},{5,10},{6,11},{8,13},{9,14},{10,15},{16,21... | collective-permute-start | bytes 245768 | tf_op jit(solution)/shard_map/ppermute | solution.py:211
  5.2 6.4 %collective-permute-start = (f32[4,40,128]{2,1,0:T(8,128)S(1)}, f32[4,40,128]{2,1,0:T(8,128)S(1)}, u32[]{:S(2)}, u32[]{:S(2)}) collective-permute-start(f32[4,40,128]{2,1,0:T(8,128)S(1)} %get-tuple-element.12), channel_id=1, source_target_pairs={{0,4},{4,8},{8,12},{1,5},{5,9},{9,13},{2,6},{6,10},{10,14},{3,7},{... | collective-permute-start | bytes 245768 | tf_op jit(solution)/shard_map/ppermute | solution.py:198
  8.5 5.8 %collective-permute-start.1 = (f32[2,128,128]{2,0,1:T(2,128)S(1)}, f32[2,128,128]{2,0,1:T(2,128)S(1)}, u32[]{:S(2)}, u32[]{:S(2)}) collective-permute-start(f32[2,128,128]{2,0,1:T(2,128)S(1)} %copy.27), channel_id=1, source_target_pairs={{0,1},{1,2},{2,3},{4,5},{5,6},{6,7},{8,9},{9,10},{10,11},{12,13},{... | collective-permute-start | bytes 393224 | tf_op jit(solution)/shard_map/ppermute | solution.py:198
  11.8 14.7 %collective-permute-start.6 = (f32[168,128]{1,0:T(8,128)S(1)}, f32[168,128]{1,0:T(8,128)S(1)}, u32[]{:S(2)}, u32[]{:S(2)}) collective-permute-start(f32[168,128]{1,0:T(8,128)S(1)} %maximum_maximum_fusion), channel_id=1, source_target_pairs={{1,0},{2,1},{3,2},{5,4},{6,5},{7,6},{9,8},{10,9},{11,10},{13,12},{... | collective-permute-start | bytes 258056 | tf_op jit(solution)/shard_map/ppermute | solution.py:198
  14.4 12.1 %copy-start.3 = (f32[4,3]{1,0:T(4,128)S(1)}, f32[4,3]{1,0:T(4,128)}, u32[]{:S(2)}) copy-start(f32[4,3]{1,0:T(4,128)} %light_ref.1) | copy-start | bytes 148
  14.4 12.1 %collective-permute-start.4 = (f32[2,168,128]{2,1,0:T(8,128)S(1)}, f32[2,168,128]{2,1,0:T(8,128)S(1)}, u32[]{:S(2)}, u32[]{:S(2)}) collective-permute-start(f32[2,168,128]{2,1,0:T(8,128)S(1)} %get-tuple-element.17), channel_id=1, source_target_pairs={{16,32},{32,16},{48,64},{64,48},{80,96},{96,80},{112,128},{128,112... | collective-permute-start | bytes 516104 | tf_op jit(solution)/shard_map/ppermute | solution.py:203
  20.2 6.3 %collective-permute-start.3 = (f32[2,168,128]{2,1,0:T(8,128)S(1)}, f32[2,168,128]{2,1,0:T(8,128)S(1)}, u32[]{:S(2)}, u32[]{:S(2)}) collective-permute-start(f32[2,168,128]{2,1,0:T(8,128)S(1)} %get-tuple-element.18), channel_id=1, source_target_pairs={{0,16},{16,0},{32,48},{48,32},{64,80},{80,64},{96,112},{112,96},{1... | collective-permute-start | bytes 516104 | tf_op jit(solution)/shard_map/ppermute | solution.py:203
  22.1 4.4 %collective-permute-start.5 = (f32[6,128]{1,0:T(8,128)S(1)}, f32[6,128]{1,0:T(8,128)S(1)}, u32[]{:S(2)}, u32[]{:S(2)}) collective-permute-start(f32[6,128]{1,0:T(8,128)S(1)} %pad_maximum_fusion.4), channel_id=1, source_target_pairs={{4,0},{8,4},{12,8},{5,1},{9,5},{13,9},{6,2},{10,6},{14,10},{7,3},{... | collective-permute-start | bytes 9224 | tf_op jit(solution)/shard_map/ppermute | solution.py:198
  26.5 73.2 %copy-start.4 = (s32[4,32]{1,0:T(4,128)S(1)}, s32[4,32]{1,0:T(4,128)}, u32[]{:S(2)}) copy-start(s32[4,32]{1,0:T(4,128)} %order_ref.1) | copy-start | bytes 1540

commit v6 on v5

--- a/solution.py
+++ b/solution.py
@@ -103,17 +103,12 @@
             store_strips(pieces_ref, base, 48 + view * 4, depth * inside)
 
 
-def render_kernel(
-    shear_ref, offset_ref, light_ref,
-    started_ref, tones_ref, cells_ref, inner_ref, outer_ref, below_ref, right_ref,
-    pieces_ref,
-    normals,
-):
+def make_normals(tiles, cells_ref, inner_ref, outer_ref, below_ref, right_ref, normals):
     lane8 = lax.broadcasted_iota(jnp.int32, (8, TILE), 1)
     row8 = lax.broadcasted_iota(jnp.int32, (8, TILE), 0)
     even = jnp.full((8, TILE), lax.axis_index("gz"), jnp.int32) % 2 == 0
 
-    for i in range(EXT // 8):
+    for i in tiles:
         row = slice(8 * i, 8 * i + 8)
         cells = [[cells_ref[k, half, row] for half in range(2)] for k in range(BZ)]
         inner = [inner_ref[half, row] for half in range(2)]
@@ -155,6 +150,19 @@
                 normals[1, k, half, row] = gr * factor
                 normals[2, k, half, row] = gc * factor
 
+
+def normals_kernel(cells_ref, inner_ref, outer_ref, right_ref, normals):
+    tiles = range(EXT // 8 - 1)
+    make_normals(tiles, cells_ref, inner_ref, outer_ref, None, right_ref, normals)
+
+
+def render_kernel(
+    shear_ref, offset_ref, light_ref,
+    started_ref, made_ref, tones_ref, cells_ref, inner_ref, outer_ref, below_ref, right_ref,
+    pieces_ref, normals,
+):
+    tiles = (EXT // 8 - 1,)
+    make_normals(tiles, cells_ref, inner_ref, outer_ref, below_ref, right_ref, normals)
     moves, _ = moves_of(shear_ref, offset_ref)
     for view in range(VIEWS):
         ld = jnp.full((8, TILE), light_ref[view, 0], jnp.float32)
@@ -261,16 +269,25 @@
         ),
         name="tone",
     )(shears, offsets, palette.T, rate[None], own, above, left, corner)
-    (pieces,) = pl.pallas_call(
+    normals_shape = (3, BZ, 2, EXT, TILE)
+    (normals,) = pl.pallas_call(
+        normals_kernel,
+        out_shape=shapes(normals_shape),
+        in_specs=[VMEM] * 4,
+        out_specs=[VMEM],
+        compiler_params=SMALL,
+        cost_estimate=pl.CostEstimate(flops=10**7, bytes_accessed=4 * 10**6, transcendentals=10**6),
+        name="normals",
+    )(cells, inner, outer, right)
+    pieces, _ = pl.pallas_call(
         render_kernel,
-        out_shape=shapes(strips_shape),
-        in_specs=[VMEM] * 10,
-        out_specs=[VMEM],
-        input_output_aliases={3: 0},
-        scratch_shapes=[pltpu.VMEM((3, BZ, 2, EXT, TILE), jnp.float32)],
+        out_shape=shapes(strips_shape, normals_shape),
+        in_specs=[VMEM] * 11,
+        out_specs=[VMEM] * 2,
+        input_output_aliases={3: 0, 4: 1},
         compiler_params=MEDIUM,
         name="render",
-    )(shears, offsets, light, pieces, tones, cells, inner, outer, below, right)
+    )(shears, offsets, light, pieces, normals, tones, cells, inner, outer, below, right)
 
     strips = lax.all_to_all(pieces, "gz", 0, 0, tiled=True)
 

time: 101 us -> 101 us (level)
  no operation moved by 1% of the time
where the time goes in v6:
time: 101 us; the launch traced here: 100 us
  blocking collectives  71.5 us (71%)
  starting transfers between devices  21.6 us (21%)
  Pallas kernels  4.61 us (5%)
  local copies, waits for them, and re-layouts  1.38 us (1%)
    all_to_all x1, blocking collectives, on_device(): strips = lax.all_to_all(pieces, 'gz', 0, 0, tiled=True)  71.5 us
    ppermute x4, starting transfers between devices, moved(): lax.ppermute(value, axes, [(i, i + steps) for i in range(first, last)])  9.78 us
    ppermute x2, starting transfers between devices, swapped(): lax.ppermute(value, axis, [p for i in lows for p in ((i, i + 1), (i + 1,...  7.65 us
    ppermute x1, starting transfers between devices, diagonal(): return lax.ppermute(value, ('gy', 'gx'), pairs)  4.13 us
  transfers between devices with their start and end apart: 7, of which 1 were waited for; matrix products, arithmetic and copies ran while one was open for 1% of the time, Pallas kernels for 2%

profile of v6, /device:TPU:3, one launch (start us, length us, event | category | flops | bytes accessed | tf_op | source)
XLA Modules:
  0.0 100.2 jit_solution(16001508534417419752)
XLA Ops:
  0.0 0.9 copy-done
  1.0 0.1 pack.1
  1.1 4.1 %collective-permute-start.2 = (f32[4,40,128]{2,1,0:T(8,128)S(1)}, f32[4,40,128]{2,1,0:T(8,128)S(1)}, u32[]{:S(2)}, u32[]{:S(2)}) collective-permute-start(f32[4,40,128]{2,1,0:T(8,128)S(1)} %get-tuple-element.13), channel_id=1, source_target_pairs={{0,5},{1,6},{2,7},{4,9},{5,10},{6,11},{8,13},{9,14},{10,15},{16,21... | collective-permute-start | bytes 245768 | tf_op jit(solution)/shard_map/ppermute | solution.py:219
  5.2 3.2 %collective-permute-start = (f32[4,40,128]{2,1,0:T(8,128)S(1)}, f32[4,40,128]{2,1,0:T(8,128)S(1)}, u32[]{:S(2)}, u32[]{:S(2)}) collective-permute-start(f32[4,40,128]{2,1,0:T(8,128)S(1)} %get-tuple-element.13), channel_id=1, source_target_pairs={{0,4},{4,8},{8,12},{1,5},{5,9},{9,13},{2,6},{6,10},{10,14},{3,7},{... | collective-permute-start | bytes 245768 | tf_op jit(solution)/shard_map/ppermute | solution.py:206
  8.4 0.0 copy-start.1
  8.4 0.0 copy-start.2
  8.4 0.0 copy-start.5
  8.4 0.0 copy-start.6
  8.5 0.1 copy.28
  8.6 2.8 %collective-permute-start.1 = (f32[2,128,128]{2,0,1:T(2,128)S(1)}, f32[2,128,128]{2,0,1:T(2,128)S(1)}, u32[]{:S(2)}, u32[]{:S(2)}) collective-permute-start(f32[2,128,128]{2,0,1:T(2,128)S(1)} %copy.28), channel_id=1, source_target_pairs={{0,1},{1,2},{2,3},{4,5},{5,6},{6,7},{8,9},{9,10},{10,11},{12,13},{... | collective-permute-start | bytes 393224 | tf_op jit(solution)/shard_map/ppermute | solution.py:206
  11.4 0.2 copy.30
  11.7 0.1 maximum_maximum_fusion
  11.8 2.5 %collective-permute-start.5 = (f32[168,128]{1,0:T(8,128)S(1)}, f32[168,128]{1,0:T(8,128)S(1)}, u32[]{:S(2)}, u32[]{:S(2)}) collective-permute-start(f32[168,128]{1,0:T(8,128)S(1)} %maximum_maximum_fusion), channel_id=1, source_target_pairs={{1,0},{2,1},{3,2},{5,4},{6,5},{7,6},{9,8},{10,9},{11,10},{13,12},{... | collective-permute-start | bytes 258056 | tf_op jit(solution)/shard_map/ppermute | solution.py:206
  14.5 5.7 %collective-permute-start.4 = (f32[2,168,128]{2,1,0:T(8,128)S(1)}, f32[2,168,128]{2,1,0:T(8,128)S(1)}, u32[]{:S(2)}, u32[]{:S(2)}) collective-permute-start(f32[2,168,128]{2,1,0:T(8,128)S(1)} %get-tuple-element.19), channel_id=1, source_target_pairs={{16,32},{32,16},{48,64},{64,48},{80,96},{96,80},{112,128},{128,112... | collective-permute-start | bytes 516104 | tf_op jit(solution)/shard_map/ppermute | solution.py:211
  20.2 1.9 %collective-permute-start.3 = (f32[2,168,128]{2,1,0:T(8,128)S(1)}, f32[2,168,128]{2,1,0:T(8,128)S(1)}, u32[]{:S(2)}, u32[]{:S(2)}) collective-permute-start(f32[2,168,128]{2,1,0:T(8,128)S(1)} %get-tuple-element.20), channel_id=1, source_target_pairs={{0,16},{16,0},{32,48},{48,32},{64,80},{80,64},{96,112},{112,96},{1... | collective-permute-start | bytes 516104 | tf_op jit(solution)/shard_map/ppermute | solution.py:211
  22.2 1.3 %collective-permute-start.6 = (f32[6,128]{1,0:T(8,128)S(1)}, f32[6,128]{1,0:T(8,128)S(1)}, u32[]{:S(2)}, u32[]{:S(2)}) collective-permute-start(f32[6,128]{1,0:T(8,128)S(1)} %pad_maximum_fusion.4), channel_id=1, source_target_pairs={{4,0},{8,4},{12,8},{5,1},{9,5},{13,9},{6,2},{10,6},{14,10},{7,3},{... | collective-permute-start | bytes 9224 | tf_op jit(solution)/shard_map/ppermute | solution.py:206
  23.5 1.8 %tone.1 = (f32[32,64,128]{2,1,0:T(8,128)S(1)}, f32[4,4,3,128,128]{4,3,2,1,0:T(8,128)S(1)}, f32[4,2,168,128]{3,2,1,0:T(8,128)S(1)}) custom-call(s32[4,2,128]{2,1,0:T(2,128)S(1)} %bitcast.45, s32[4,2,32]{2,1,0:T(2,128)S(1)} %bitcast.47, f32[2,3]{1,0:T(2,128)S(1)} %bitcast.49, f32[1,4]{1,0:T(1,128)S(1)} %bitcast.50, ...), custom_call_target="tpu_custom_call" | custom-call | flops 10000000 | bytes 4000000 | tf_op jit(solution)/shard_map/tone/pallas_call | solution.py:260
  25.3 0.0 copy-start.4
  25.4 0.5 normals.1.made_ref
  25.9 0.6 collective-permute-done.6.below_ref
  26.5 1.3 %render.1 = (f32[32,64,128]{2,1,0:T(8,128)S(1)}, f32[3,4,2,168,128]{4,3,2,1,0:T(8,128)S(1)}) custom-call(s32[4,2,128]{2,1,0:T(2,128)S(1)} %bitcast.46, s32[4,2,32]{2,1,0:T(2,128)S(1)} %bitcast.48, f32[4,3]{1,0:T(4,128)S(1)} %copy-done.4, f32[32,64,128]{2,1,0:T(8,128)S(1)} %get-tuple-element.15.started_ref, ...), custom_call_target="tpu_custom_call", output_to_operand_aliasing={{0}: (3, {}), {1}: (4, {})} | custom-call | tf_op jit(solution)/shard_map/render/pallas_call | solution.py:282
  27.8 0.0 copy-start.3
  27.8 71.5 %all_to_all.5.pieces_ref = f32[32,64,128]{2,1,0:T(8,128)S(1)} all-to-all(f32[32,64,128]{2,1,0:T(8,128)S(1)} %get-tuple-element.18), channel_id=1, replica_groups=mesh['gz'=32,'gy'=4,'gx'=4] {'gz'}, dimensions={0} | all-to-all | bytes 2097152 | tf_op jit(solution)/shard_map/all_to_all | solution.py:292
  99.3 0.9 composite.1
  (26 shorter events, 0.2 us)
Async XLA Ops:
  0.0 0.9 copy-start
  1.1 13.2 %collective-permute-start.2 = (f32[4,40,128]{2,1,0:T(8,128)S(1)}, f32[4,40,128]{2,1,0:T(8,128)S(1)}, u32[]{:S(2)}, u32[]{:S(2)}) collective-permute-start(f32[4,40,128]{2,1,0:T(8,128)S(1)} %get-tuple-element.13), channel_id=1, source_target_pairs={{0,5},{1,6},{2,7},{4,9},{5,10},{6,11},{8,13},{9,14},{10,15},{16,21... | collective-permute-start | bytes 245768 | tf_op jit(solution)/shard_map/ppermute | solution.py:219
  5.2 6.5 %collective-permute-start = (f32[4,40,128]{2,1,0:T(8,128)S(1)}, f32[4,40,128]{2,1,0:T(8,128)S(1)}, u32[]{:S(2)}, u32[]{:S(2)}) collective-permute-start(f32[4,40,128]{2,1,0:T(8,128)S(1)} %get-tuple-element.13), channel_id=1, source_target_pairs={{0,4},{4,8},{8,12},{1,5},{5,9},{9,13},{2,6},{6,10},{10,14},{3,7},{... | collective-permute-start | bytes 245768 | tf_op jit(solution)/shard_map/ppermute | solution.py:206
  8.4 15.1 %copy-start.1 = (s32[4,128,2]{1,2,0:T(2,128)S(1)}, s32[4,128,2]{1,2,0:T(2,128)}, u32[]{:S(2)}) copy-start(s32[4,128,2]{1,2,0:T(2,128)} %param.11) | copy-start | bytes 12292
  8.4 15.1 %copy-start.2 = (s32[4,32,2]{1,2,0:T(2,128)S(1)}, s32[4,32,2]{1,2,0:T(2,128)}, u32[]{:S(2)}) copy-start(s32[4,32,2]{1,2,0:T(2,128)} %param.12) | copy-start | bytes 3076
  8.4 15.1 %copy-start.5 = (f32[3,2]{0,1:T(2,128)S(1)}, f32[3,2]{0,1:T(2,128)}, u32[]{:S(2)}) copy-start(f32[3,2]{0,1:T(2,128)} %param.9) | copy-start | bytes 76
  8.4 15.1 %copy-start.6 = (f32[4]{0:T(128)S(1)}, f32[4]{0:T(128)}, u32[]{:S(2)}) copy-start(f32[4]{0:T(128)} %param.10) | copy-start | bytes 52
  8.6 5.8 %collective-permute-start.1 = (f32[2,128,128]{2,0,1:T(2,128)S(1)}, f32[2,128,128]{2,0,1:T(2,128)S(1)}, u32[]{:S(2)}, u32[]{:S(2)}) collective-permute-start(f32[2,128,128]{2,0,1:T(2,128)S(1)} %copy.28), channel_id=1, source_target_pairs={{0,1},{1,2},{2,3},{4,5},{5,6},{6,7},{8,9},{9,10},{10,11},{12,13},{... | collective-permute-start | bytes 393224 | tf_op jit(solution)/shard_map/ppermute | solution.py:206
  11.8 13.5 %collective-permute-start.5 = (f32[168,128]{1,0:T(8,128)S(1)}, f32[168,128]{1,0:T(8,128)S(1)}, u32[]{:S(2)}, u32[]{:S(2)}) collective-permute-start(f32[168,128]{1,0:T(8,128)S(1)} %maximum_maximum_fusion), channel_id=1, source_target_pairs={{1,0},{2,1},{3,2},{5,4},{6,5},{7,6},{9,8},{10,9},{11,10},{13,12},{... | collective-permute-start | bytes 258056 | tf_op jit(solution)/shard_map/ppermute | solution.py:206
  14.5 10.9 %collective-permute-start.4 = (f32[2,168,128]{2,1,0:T(8,128)S(1)}, f32[2,168,128]{2,1,0:T(8,128)S(1)}, u32[]{:S(2)}, u32[]{:S(2)}) collective-permute-start(f32[2,168,128]{2,1,0:T(8,128)S(1)} %get-tuple-element.19), channel_id=1, source_target_pairs={{16,32},{32,16},{48,64},{64,48},{80,96},{96,80},{112,128},{128,112... | collective-permute-start | bytes 516104 | tf_op jit(solution)/shard_map/ppermute | solution.py:211
  20.2 5.2 %collective-permute-start.3 = (f32[2,168,128]{2,1,0:T(8,128)S(1)}, f32[2,168,128]{2,1,0:T(8,128)S(1)}, u32[]{:S(2)}, u32[]{:S(2)}) collective-permute-start(f32[2,168,128]{2,1,0:T(8,128)S(1)} %get-tuple-element.20), channel_id=1, source_target_pairs={{0,16},{16,0},{32,48},{48,32},{64,80},{80,64},{96,112},{112,96},{1... | collective-permute-start | bytes 516104 | tf_op jit(solution)/shard_map/ppermute | solution.py:211
  22.2 4.4 %collective-permute-start.6 = (f32[6,128]{1,0:T(8,128)S(1)}, f32[6,128]{1,0:T(8,128)S(1)}, u32[]{:S(2)}, u32[]{:S(2)}) collective-permute-start(f32[6,128]{1,0:T(8,128)S(1)} %pad_maximum_fusion.4), channel_id=1, source_target_pairs={{4,0},{8,4},{12,8},{5,1},{9,5},{13,9},{6,2},{10,6},{14,10},{7,3},{... | collective-permute-start | bytes 9224 | tf_op jit(solution)/shard_map/ppermute | solution.py:206
  25.3 1.2 %copy-start.4 = (f32[4,3]{1,0:T(4,128)S(1)}, f32[4,3]{1,0:T(4,128)}, u32[]{:S(2)}) copy-start(f32[4,3]{1,0:T(4,128)} %light_ref.1) | copy-start | bytes 148
  27.8 71.5 %copy-start.3 = (s32[4,32]{1,0:T(4,128)S(1)}, s32[4,32]{1,0:T(4,128)}, u32[]{:S(2)}) copy-start(s32[4,32]{1,0:T(4,128)} %order_ref.1) | copy-start | bytes 1540
